TPU v7x, 256 devices: a whole 4x4x8 slice. The times are simulated.
256 devices in a mesh: band: 32 (over x_hi, z, core), tm: 8 (over x_lo, y).
Axes of the slice: x: 4 (x_hi: 2, x_lo: 2; x = x_hi * 2 + x_lo), y: 4, z: 8, core: 2. Of those that a mesh axis runs over, the one named last changes fastest.
Arguments:
- intensity: bfloat16 [16384, 8192], P('band', 'tm')
- shifts: int32 [12, 4096], P(None, 'band'), may hold values from 0 to 32, as said below
- boxcar_widths: int32 [8], replicated, may hold values from 1 to 64, as said below
Outputs:
- dedispersed: float32 [4096, 8192], P('band', 'tm')
- peak_snr: float32 [4096, 8192], P('band', 'tm')
Inputs may be any that keep to these rules, and one draw needn't show every extreme that they name: Every section s has some entry shifts[s, n] equal to 32. `boxcar_widths`: one of the widths equals 64; widths may repeat.
All inputs are finite; a program needn't handle non-finite values.
Results may differ from a plain program's by a relative error of at most 0.0003.
Values sent between devices are 32-bit elements; how exact they have to be, the bound alone decides.
A program may use at most 64 MiB of HBM per device.

v0:
```python
import jax
import jax.numpy as jnp
from jax import lax
from jax.experimental import pallas as pl
from jax.experimental.pallas import tpu as pltpu
from jax.sharding import PartitionSpec as P

MESH = pl.DeviceIdType.MESH
F32, BF16, I32 = jnp.float32, jnp.bfloat16, jnp.int32
NB, NT = 32, 8
NBOX = 8
NCOL = 16
LOCAL, CROSS = 7, 5
TILES = 4
SAMPLES = 8192

_ROWS = lax.GatherDimensionNumbers(
    offset_dims=(),
    collapsed_slice_dims=(1,),
    start_index_map=(1,),
    operand_batching_dims=(0,),
    start_indices_batching_dims=(0,),
)


def iota(shape, dim):
    return lax.broadcasted_iota(I32, shape, dim)


def take_lanes(x, index):
    return lax.gather(
        x, index[..., None], _ROWS, (1, 1), mode=lax.GatherScatterMode.PROMISE_IN_BOUNDS
    )


def rev5(v):
    out = 0
    for k in range(5):
        out = out + (v // 2**k) % 2 * 2 ** (4 - k)
    return out


OFFSETS = sorted(
    [(dx, dz, dc) for dx in range(2) for dz in range(8) for dc in range(2)][1:],
    key=lambda o: (o[0], -min(o[1], 8 - o[1])),
)


def delay_add(firsts, seconds, index, keep):
    rows, tiles = firsts.shape[:2]
    spread = jnp.broadcast_to(index[:, None], firsts.shape).reshape(-1, 128)
    turned = take_lanes(seconds.reshape(-1, 128), spread).reshape(firsts.shape)
    wraps = index > iota(index.shape, 2)
    later = tiles - max(1, tiles - keep)
    wraps = jnp.broadcast_to(wraps[:, None], (rows, later, 8, 128))
    term = jnp.where(wraps, turned[:, tiles - later - 1 : tiles - 1], turned[:, tiles - later :])
    out = firsts[:, tiles - later :] + term
    if keep == tiles:
        out = jnp.concatenate([firsts[:, :1] + turned[:, :1], out], axis=1)
    return out


def major_section(x, index, apart, keep):
    rows, tiles = x.shape[:2]
    shape = (rows // (2 * apart), 2, apart, tiles, 8, 128)
    pairs = x.reshape(shape)
    both = [jnp.broadcast_to(pairs[:, e : e + 1], shape).reshape(x.shape) for e in (0, 1)]
    return delay_add(*both, index, keep)


def minor_section(x, index, apart, keep):
    flat = x.reshape(-1, 8, 128)
    is_set = iota(flat.shape, 1) // apart % 2 == 1
    firsts = jnp.where(is_set, pltpu.roll(flat, apart, 1), flat)
    seconds = jnp.where(is_set, flat, pltpu.roll(flat, 8 - apart, 1))
    return delay_add(firsts.reshape(x.shape), seconds.reshape(x.shape), index, keep)


def swap_halves(x):
    return pltpu.roll(x.reshape(-1, 8, 128), 4, 1).reshape(x.shape)


def kernel(
    x_hbm, par_hbm, ded_ref, snr_ref,
    xc, par, shsend, shbuf, idx1, idx2, l0, s7, hsend, hrecv, gsend, grecv,
    recv, t2, hi, lo, bc, band, roots, stsend, stbuf,
    local_sem, shs_sem, shr_sem, halo_sem, a2a_send, a2a_recv, st_send, st_recv,
):
    me, t = lax.axis_index("band"), lax.axis_index("tm")
    copy_par = pltpu.make_async_copy(par_hbm, par, local_sem.at[0])
    copy_x1 = pltpu.make_async_copy(x_hbm.at[:, pl.ds(512, 512)], xc.at[pl.ds(512, 512)], local_sem.at[1])
    copy_x0 = pltpu.make_async_copy(x_hbm.at[:, pl.ds(0, 512)], xc.at[pl.ds(0, 512)], local_sem.at[2])
    copy_par.start()
    copy_x1.start()
    copy_x0.start()

    barrier = pltpu.get_barrier_semaphore()
    for i in range(1, NB):
        pl.semaphore_signal(barrier, inc=1, device_id={"band": lax.rem(me + i, NB)}, device_id_type=MESH)
    for i in range(1, NT):
        pl.semaphore_signal(barrier, inc=1, device_id={"tm": lax.rem(t + i, NT)}, device_id_type=MESH)

    column, place = me // NCOL, me % NCOL
    z, core = place // 2, place % 2
    later = lax.rem(t + 1, NT)
    slot = rev5(me)
    sub8, lane8 = iota((8, 128), 0), iota((8, 128), 1)

    def group_of(i, halves):
        blocks = i // 8 if halves else i // 4
        return blocks + 32 * (i // 2 % 2) + 64 * (i % 2)

    copy_par.wait()
    for s in range(1, LOCAL + 1):
        row = jnp.broadcast_to(par[s - 1 : s, :], (8, 128))
        if s <= 5:
            base = sub8 // 2 % 2 * 32 + sub8 % 2 * 64
        else:
            base = sub8 // 2 % 2 * (1, 2)[s - 6] + sub8 % 2 * (64, 1)[s - 6]
        for m in range(32):
            turned = int(f"{m:05b}"[::-1], 2)
            if s <= 5:
                turned = (turned >> (5 - s)) + (m >> s << s)
            else:
                turned = turned << (s - 5)
            idx1[s - 1, m] = (lane8 - take_lanes(row, base + turned)) & 127
    for j in range(CROSS - 1):
        shsend[j] = par[LOCAL + j : LOCAL + j + 1, :]
        shbuf[me, j] = par[LOCAL + j : LOCAL + j + 1, :]

    i = iota((256, 1024), 0)
    target = i // 4 % 2 * 128 + group_of(i, True)
    presum = jnp.where(iota((256, 1024), 1) // 4 == target, 1.0, 0.0).astype(BF16)
    i = iota((128, 512), 0)
    presum_edge = jnp.where(iota((128, 512), 1) // 4 == group_of(i, False), 1.0, 0.0).astype(BF16)
    copy_x1.wait()
    copy_x0.wait()
    level = jnp.dot(presum, xc[...], preferred_element_type=F32)
    for k in range(TILES):
        l0[:, 2 + k] = level[:, k * 128 : (k + 1) * 128].reshape(32, 8, 128)
    edge = jnp.dot(presum_edge, xc[512:1024, 256:512], preferred_element_type=F32)
    for k in range(2):
        hsend[k] = edge[:, k * 128 : (k + 1) * 128]

    def local_sections(first, tiles):
        x = l0[:, first : first + tiles + 2]
        for s, keep in ((1, tiles + 2), (2, tiles + 2), (3, tiles + 1), (4, tiles + 1), (5, tiles + 1)):
            x = major_section(x, idx1[s - 1], 2 ** (s - 1), keep)
        for s, keep in ((6, tiles + 1), (7, tiles)):
            x = minor_section(x, idx1[s - 1], 2 ** (7 - s), keep)
        s7[:, first : first + tiles] = x

    def part_copy(c, k):
        dx, dz, dc = OFFSETS[k]
        dest = (column + dx) % 2 * NCOL + (z + dz) % 8 * 2 + (core + dc) % 2
        return pltpu.make_async_remote_copy(
            src_ref=s7.at[dest, pl.ds(2 * c, 2)], dst_ref=recv.at[slot, pl.ds(2 + 2 * c, 2)],
            send_sem=a2a_send.at[c, k], recv_sem=a2a_recv.at[c, k],
            device_id={"band": dest}, device_id_type=MESH,
        )

    def start_parts(c, order):
        for k in order:
            part_copy(c, k).start()
        recv[slot, 2 + 2 * c : 4 + 2 * c] = s7[me, 2 * c : 2 * c + 2]

    def await_parts(c):
        for k in range(NB - 1):
            part_copy(c, k).wait_recv()

    def shift_copy(i):
        return pltpu.make_async_remote_copy(
            src_ref=shsend, dst_ref=shbuf.at[me], send_sem=shs_sem.at[i], recv_sem=shr_sem.at[i],
            device_id={"band": lax.rem(me + 2 * i, NB)}, device_id_type=MESH,
        )

    halo_copy = pltpu.make_async_remote_copy(
        src_ref=hsend, dst_ref=hrecv, send_sem=halo_sem.at[0], recv_sem=halo_sem.at[1],
        device_id={"tm": later}, device_id_type=MESH,
    )
    edge_copy = pltpu.make_async_remote_copy(
        src_ref=gsend, dst_ref=grecv, send_sem=halo_sem.at[2], recv_sem=halo_sem.at[3],
        device_id={"tm": later}, device_id_type=MESH,
    )
    has_next, has_last = t < NT - 1, t > 0

    local_sections(2, 2)
    pl.semaphore_wait(barrier, NB + NT - 2)
    pl.when(has_next)(halo_copy.start)
    for i in range(1, NB // 2):
        shift_copy(i).start()
    start_parts(1, range(NB - 1))

    before = jnp.dot(presum[:, 512:], xc[0:512, 256:512], preferred_element_type=F32)

    @pl.when(t == 0)
    def _():
        hrecv[...] = jnp.zeros((2, 128, 128), F32)
        grecv[...] = jnp.zeros((2, 128, 128), F32)

    pl.when(has_last)(halo_copy.wait_recv)
    is_low = iota((32, 8, 128), 1) < 4

    def spread_edge(packed):
        return jnp.stack([packed, swap_halves(packed)], axis=1).reshape(32, 8, 128)

    for k in range(2):
        own = before[:, k * 128 : (k + 1) * 128].reshape(32, 8, 128)
        l0[:, k] = jnp.where(is_low, spread_edge(hrecv[k].reshape(16, 8, 128)), own)
    local_sections(0, 2)
    start_parts(0, [*range(NCOL - 1, NB - 1), *range(NCOL - 1)])

    offset, sample = iota((256, 128), 0) - 128, iota((256, 128), 1)
    row = jnp.broadcast_to(par[12:13, :], (8, 128))
    for j in range(NBOX):
        width = take_lanes(row, jnp.full((8, 128), j, I32))
        root = jnp.sqrt(width.astype(F32))
        roots[0, j] = root
        roots[1, j] = 1.0 / root
        width = jnp.broadcast_to(width[None], (32, 8, 128)).reshape(256, 128)
        inside = (offset <= sample) & (offset > sample - width)
        band[:, j * 128 : (j + 1) * 128] = jnp.where(inside, 1.0, 0.0).astype(BF16)

    for i in range(1, NB // 2):
        shift_copy(i).wait_recv()
    quarter = sub8 % 4
    for j in range(1, CROSS + 1):
        base = 0
        for bit in range(j, CROSS):
            base = base + me // 2**bit % 2 * 2 ** (6 - bit + j)
        for low in range(2 ** (CROSS - j)):
            if j < CROSS:
                source = me % 2**j
                for bit in range(j, CROSS):
                    source = source + 2**bit * ((low >> (4 - bit)) & 1)
                row = shbuf[source, j - 1]
            else:
                row = par[LOCAL + j - 1 : LOCAL + j, :]
            row = jnp.broadcast_to(row, (8, 128))
            for high in range(2**j):
                delay = take_lanes(row, base + 2**j * quarter + high)
                idx2[j - 1, low + 2 ** (CROSS - j) * high] = (lane8 - delay) & 127

    await_parts(1)
    for k in range(2):
        pairs = recv[:, 4 + k].reshape(16, 2, 8, 128)
        even, odd = swap_halves(pairs[:, 0]), pairs[:, 1]
        gsend[k] = jnp.where(iota((16, 8, 128), 1) < 4, even, odd).reshape(128, 128)
    pl.when(has_next)(edge_copy.start)
    pl.when(has_last)(edge_copy.wait_recv)
    for k in range(2):
        own = swap_halves(recv[:, 4 + k])
        recv[:, k] = jnp.where(is_low, spread_edge(grecv[k].reshape(16, 8, 128)), own)

    await_parts(0)
    x = recv[...]
    for j, keep in ((1, 6), (2, 6), (3, 5), (4, 5), (5, 5)):
        x = major_section(x, idx2[j - 1], 2 ** (CROSS - j), keep)
    x = x * (16384.0 ** (-0.5))
    for k in range(5):
        t2[k] = x[:, k].reshape(256, 128)
    total = x[:, 1] + x[:, 2] + x[:, 3] + x[:, 4]
    total = jnp.sum(total + swap_halves(total), axis=2, keepdims=True)
    pivot = jnp.broadcast_to(total * (1.0 / 1024), (32, 8, 128))
    squares = jnp.zeros((32, 8, 128), F32)
    for k in range(5):
        centred = x[:, k] - pivot
        if k:
            squares = squares + centred * centred
        centred = centred.reshape(256, 128)
        high = centred.astype(BF16)
        hi[:, k * 128 : (k + 1) * 128] = high
        lo[:, k * 128 : (k + 1) * 128] = (centred - high.astype(F32)).astype(BF16)
    squares = jnp.sum(squares + swap_halves(squares), axis=2, keepdims=True)
    packed = jnp.where(iota((32, 8, 128), 2) == 0, pivot, jnp.broadcast_to(squares, (32, 8, 128)))
    mine = jnp.transpose(packed.reshape(256, 128))[0:8]
    stsend[...] = mine
    stbuf[t] = mine

    def stat_copy(i):
        return pltpu.make_async_remote_copy(
            src_ref=stsend, dst_ref=stbuf.at[t], send_sem=st_send.at[i], recv_sem=st_recv.at[i],
            device_id={"tm": lax.rem(t + i, NT)}, device_id_type=MESH,
        )

    for i in range(1, NT):
        stat_copy(i).start()

    def unmix(source, first, out):
        for k in range(TILES):
            for s in range(8):
                for b in range(4):
                    rows = source[first + k, pl.ds(b * 64 + s, 8, stride=8), :]
                    out[pl.ds(s % 4 * 32 + b * 8, 8), pl.ds(s // 4 * 512 + k * 128, 128)] = rows

    unmix(t2, 1, ded_ref)
    for k in range(TILES):
        at = pl.ds(k * 128, 256)
        both = jnp.dot(hi[:, at], band[...], preferred_element_type=F32)
        bc[k] = both + jnp.dot(lo[:, at], band[...], preferred_element_type=F32)

    for c in range(2):
        for k in range(NB - 1):
            part_copy(c, k).wait_send()
    for i in range(1, NB // 2):
        shift_copy(i).wait_send()
    pl.when(has_next)(halo_copy.wait_send)
    pl.when(has_next)(edge_copy.wait_send)
    for i in range(1, NT):
        stat_copy(i).wait_recv()
    means = [stbuf[i][0:1] for i in range(NT)]
    mean = sum(means) * (1.0 / NT)
    centred = [stbuf[i][1:2] + 1024.0 * ((m - mean) * (m - mean)) for i, m in enumerate(means)]
    scale = 1.0 / jnp.sqrt(sum(centred) * (1.0 / SAMPLES) + 1e-6)
    row_of = iota((8, 256), 0)
    shared = jnp.where(row_of == 0, jnp.broadcast_to(mean, (8, 256)), jnp.broadcast_to(scale, (8, 256)))
    shared = jnp.transpose(shared)
    row_mean = jnp.broadcast_to(shared[:, 0:1], (256, 128))
    row_scale = jnp.broadcast_to(shared[:, 1:2], (256, 128))
    off = pivot.reshape(256, 128) - row_mean
    for h in range(4):
        at = pl.ds(64 * h, 64)
        best = [None] * TILES
        for j in range(NBOX):
            up, down = (jnp.broadcast_to(roots[e, j][None], (8, 8, 128)).reshape(64, 128) for e in range(2))
            bias = up * off[64 * h : 64 * h + 64]
            for k in range(TILES):
                score = bc[k, at, j * 128 : (j + 1) * 128] * down + bias
                best[k] = score if j == 0 else jnp.maximum(best[k], score)
        for k in range(TILES):
            t2[k, at] = best[k] * row_scale[64 * h : 64 * h + 64]
    unmix(t2, 0, snr_ref)
    for i in range(1, NT):
        stat_copy(i).wait_send()


def store(a, b, a_hbm, b_hbm, sem):
    copies = [pltpu.make_async_copy(a, a_hbm, sem.at[0]), pltpu.make_async_copy(b, b_hbm, sem.at[1])]
    for copy in copies:
        copy.start()
    for copy in copies:
        copy.wait()


def body(intensity, shifts, boxcar_widths):
    dma = pltpu.SemaphoreType.DMA
    vmem, whole = pltpu.VMEM, pl.BlockSpec(memory_space=pl.ANY)
    in_vmem = pl.BlockSpec(memory_space=pltpu.VMEM)
    out = jax.ShapeDtypeStruct((128, 1024), F32)
    widths = jnp.pad(boxcar_widths[None], ((12, 3), (0, 128 - NBOX)))
    params = jnp.pad(shifts, ((0, 4), (0, 0))) + widths
    ded, snr = pl.pallas_call(
        kernel,
        out_shape=(out, out),
        in_specs=[whole] * 2,
        out_specs=[in_vmem] * 2,
        scratch_shapes=[
            vmem((1024, 512), BF16),
            vmem((16, 128), I32),
            vmem((4, 1, 128), I32),
            vmem((NB, 4, 1, 128), I32),
            vmem((LOCAL, 32, 8, 128), I32),
            vmem((CROSS, 32, 8, 128), I32),
            vmem((32, 6, 8, 128), F32),
            vmem((32, TILES, 8, 128), F32),
            vmem((2, 128, 128), F32),
            vmem((2, 128, 128), F32),
            vmem((2, 128, 128), F32),
            vmem((2, 128, 128), F32),
            vmem((32, 2 + TILES, 8, 128), F32),
            vmem((5, 256, 128), F32),
            vmem((256, 640), BF16),
            vmem((256, 640), BF16),
            vmem((TILES, 256, 1024), F32),
            vmem((256, 1024), BF16),
            vmem((2, NBOX, 8, 128), F32),
            vmem((8, 256), F32),
            vmem((NT, 8, 256), F32),
            dma((3,)),
            dma((NB // 2,)),
            dma((NB // 2,)),
            dma((4,)),
            dma((2, NB - 1)),
            dma((2, NB - 1)),
            dma((NT,)),
            dma((NT,)),
        ],
        compiler_params=pltpu.CompilerParams(
            collective_id=0, has_side_effects=True, vmem_limit_bytes=52 * 2**20
        ),
    )(intensity, params)
    return pl.pallas_call(
        store,
        out_shape=(out, out),
        in_specs=[in_vmem] * 2,
        out_specs=[whole] * 2,
        scratch_shapes=[dma((2,))],
        compiler_params=pltpu.CompilerParams(vmem_limit_bytes=52 * 2**20),
    )(ded, snr)


def solution(mesh):
    assert mesh.shape["band"] == NB and mesh.shape["tm"] == NT
    in_specs = (P("band", "tm"), P(None, "band"), P())
    out_specs = (P("band", "tm"), P("band", "tm"))
    return jax.shard_map(body, mesh=mesh, in_specs=in_specs, out_specs=out_specs, check_vma=False)
```

profile of v0, /device:TPU:1, one launch (start us, length us, event | category | flops | bytes accessed | tf_op | source)
XLA Modules:
  0.0 37.8 jit_solution(15247292880339284138)
XLA Ops:
  0.6 0.0 copy-start
  0.6 0.6 %copy-done = s32[8]{0:T(128)S(1)} copy-done((s32[8]{0:T(128)S(1)}, s32[8]{0:T(128)}, u32[]{:S(2)}) %copy-start) | copy-done | bytes 56
  1.3 0.7 %pad_add_fusion.par_hbm = s32[16,128]{1,0:T(8,128)S(1)} fusion(s32[1,8]{1,0:T(1,128)S(1)} %bitcast.1, s32[12,128]{1,0:T(8,128)} %param.4), kind=kLoop, calls=%fused_computation | loop fusion | flops 2048 | bytes 14368 | tf_op jit(solution)/shard_map/add | solution.py:351
  2.0 34.8 %shard_map.50 = (f32[128,1024]{1,0:T(8,128)S(1)}, f32[128,1024]{1,0:T(8,128)S(1)}) custom-call(bf16[512,1024]{1,0:T(8,128)(2,1)} %x_hbm.1, s32[16,128]{1,0:T(8,128)S(1)} %pad_add_fusion.par_hbm), custom_call_target="tpu_custom_call" | custom-call | tf_op jit(solution)/shard_map/pallas_call | solution.py:352
  36.8 1.0 %shard_map.51 = (f32[128,1024]{1,0:T(8,128)}, f32[128,1024]{1,0:T(8,128)}) custom-call(f32[128,1024]{1,0:T(8,128)S(1)} %get-tuple-element.4.a, f32[128,1024]{1,0:T(8,128)S(1)} %get-tuple-element.5.b), custom_call_target="tpu_custom_call" | custom-call | tf_op jit(solution)/shard_map/pallas_call | solution.py:392
Async XLA Ops:
  0.6 0.7 %copy-start = (s32[8]{0:T(128)S(1)}, s32[8]{0:T(128)}, u32[]{:S(2)}) copy-start(s32[8]{0:T(128)} %param.5) | copy-start | bytes 100
where the time goes:
time: 37.9 us; the launch traced here: 37.8 us
  Pallas kernels  35.8 us (94%)
  other arithmetic  0.7 us (2%)
  local copies, waits for them, and re-layouts  0.65 us (2%)
  between operations  0.65 us (2%)
    pallas_call x1, Pallas kernels, body(): pl.pallas_call(kernel, out_shape=(out, out), in_specs=[whole] * 2, out_sp...  34.8 us
    pallas_call x1, Pallas kernels, body(): pl.pallas_call(store, out_shape=(out, out), in_specs=[in_vmem] * 2, out_s...  0.99 us

commit v1 on v0

--- a/solution.py
+++ b/solution.py
@@ -46,34 +46,34 @@
 )
 
 
-def delay_add(firsts, seconds, index, keep):
-    rows, tiles = firsts.shape[:2]
+def delay_add(firsts, seconds, index, ahead=None):
     spread = jnp.broadcast_to(index[:, None], firsts.shape).reshape(-1, 128)
     turned = take_lanes(seconds.reshape(-1, 128), spread).reshape(firsts.shape)
-    wraps = index > iota(index.shape, 2)
-    later = tiles - max(1, tiles - keep)
-    wraps = jnp.broadcast_to(wraps[:, None], (rows, later, 8, 128))
-    term = jnp.where(wraps, turned[:, tiles - later - 1 : tiles - 1], turned[:, tiles - later :])
-    out = firsts[:, tiles - later :] + term
-    if keep == tiles:
-        out = jnp.concatenate([firsts[:, :1] + turned[:, :1], out], axis=1)
-    return out
-
-
-def major_section(x, index, apart, keep):
+    last = turned[:, -1:]
+    if ahead is not None:
+        before = jnp.concatenate([ahead, turned[:, :-1]], axis=1)
+    elif firsts.shape[1] == 1:
+        return firsts + turned, last
+    else:
+        before = jnp.concatenate([turned[:, :1], turned[:, :-1]], axis=1)
+    wraps = jnp.broadcast_to((index > iota(index.shape, 2))[:, None], firsts.shape)
+    return firsts + jnp.where(wraps, before, turned), last
+
+
+def major_section(x, index, apart, ahead=None):
     rows, tiles = x.shape[:2]
     shape = (rows // (2 * apart), 2, apart, tiles, 8, 128)
     pairs = x.reshape(shape)
     both = [jnp.broadcast_to(pairs[:, e : e + 1], shape).reshape(x.shape) for e in (0, 1)]
-    return delay_add(*both, index, keep)
-
-
-def minor_section(x, index, apart, keep):
+    return delay_add(*both, index, ahead)
+
+
+def minor_section(x, index, apart):
     flat = x.reshape(-1, 8, 128)
     is_set = iota(flat.shape, 1) // apart % 2 == 1
     firsts = jnp.where(is_set, pltpu.roll(flat, apart, 1), flat)
     seconds = jnp.where(is_set, flat, pltpu.roll(flat, 8 - apart, 1))
-    return delay_add(firsts.reshape(x.shape), seconds.reshape(x.shape), index, keep)
+    return delay_add(firsts.reshape(x.shape), seconds.reshape(x.shape), index)
 
 
 def swap_halves(x):
@@ -81,16 +81,14 @@
 
 
 def kernel(
-    x_hbm, par_hbm, ded_ref, snr_ref,
-    xc, par, shsend, shbuf, idx1, idx2, l0, s7, hsend, hrecv, gsend, grecv,
-    recv, t2, hi, lo, bc, band, roots, stsend, stbuf,
-    local_sem, shs_sem, shr_sem, halo_sem, a2a_send, a2a_recv, st_send, st_recv,
+    x_hbm, par, ded_ref, snr_ref,
+    xc, shsend, shbuf, idx1, idx2, l0, s7, hsend, hrecv, gsend, grecv, fsend, frecv,
+    recv, extra, t2, hi, lo, bc, band, roots, stsend, stbuf,
+    local_sem, shs_sem, shr_sem, halo_sem, back_send, back_recv, front_send, front_recv, st_send, st_recv,
 ):
     me, t = lax.axis_index("band"), lax.axis_index("tm")
-    copy_par = pltpu.make_async_copy(par_hbm, par, local_sem.at[0])
-    copy_x1 = pltpu.make_async_copy(x_hbm.at[:, pl.ds(512, 512)], xc.at[pl.ds(512, 512)], local_sem.at[1])
-    copy_x0 = pltpu.make_async_copy(x_hbm.at[:, pl.ds(0, 512)], xc.at[pl.ds(0, 512)], local_sem.at[2])
-    copy_par.start()
+    copy_x1 = pltpu.make_async_copy(x_hbm.at[:, pl.ds(512, 512)], xc.at[pl.ds(512, 512)], local_sem.at[0])
+    copy_x0 = pltpu.make_async_copy(x_hbm.at[:, pl.ds(0, 512)], xc.at[pl.ds(0, 512)], local_sem.at[1])
     copy_x1.start()
     copy_x0.start()
 
@@ -110,7 +108,6 @@
         blocks = i // 8 if halves else i // 4
         return blocks + 32 * (i // 2 % 2) + 64 * (i % 2)
 
-    copy_par.wait()
     for s in range(1, LOCAL + 1):
         row = jnp.broadcast_to(par[s - 1 : s, :], (8, 128))
         if s <= 5:
@@ -140,33 +137,46 @@
         l0[:, 2 + k] = level[:, k * 128 : (k + 1) * 128].reshape(32, 8, 128)
     edge = jnp.dot(presum_edge, xc[512:1024, 256:512], preferred_element_type=F32)
     for k in range(2):
-        hsend[k] = edge[:, k * 128 : (k + 1) * 128]
-
-    def local_sections(first, tiles):
-        x = l0[:, first : first + tiles + 2]
-        for s, keep in ((1, tiles + 2), (2, tiles + 2), (3, tiles + 1), (4, tiles + 1), (5, tiles + 1)):
-            x = major_section(x, idx1[s - 1], 2 ** (s - 1), keep)
-        for s, keep in ((6, tiles + 1), (7, tiles)):
-            x = minor_section(x, idx1[s - 1], 2 ** (7 - s), keep)
-        s7[:, first : first + tiles] = x
-
-    def part_copy(c, k):
+        hsend[:, k] = edge[:, k * 128 : (k + 1) * 128].reshape(16, 8, 128)
+
+    def local_sections(first):
+        x = l0[:, first : first + 4]
+        for s in range(1, LOCAL + 1):
+            if s <= 5:
+                x = major_section(x, idx1[s - 1], 2 ** (s - 1))[0]
+            else:
+                x = minor_section(x, idx1[s - 1], 2 ** (7 - s))[0]
+            if s in (3, 7):
+                x = x[:, 1:]
+        return x
+
+    def dest_of(k):
         dx, dz, dc = OFFSETS[k]
-        dest = (column + dx) % 2 * NCOL + (z + dz) % 8 * 2 + (core + dc) % 2
+        return (column + dx) % 2 * NCOL + (z + dz) % 8 * 2 + (core + dc) % 2
+
+    def back_copy(k):
+        dest = dest_of(k)
         return pltpu.make_async_remote_copy(
-            src_ref=s7.at[dest, pl.ds(2 * c, 2)], dst_ref=recv.at[slot, pl.ds(2 + 2 * c, 2)],
-            send_sem=a2a_send.at[c, k], recv_sem=a2a_recv.at[c, k],
+            src_ref=s7.at[dest], dst_ref=recv.at[slot // 2, slot % 2],
+            send_sem=back_send.at[k], recv_sem=back_recv.at[k],
             device_id={"band": dest}, device_id_type=MESH,
         )
 
-    def start_parts(c, order):
-        for k in order:
-            part_copy(c, k).start()
-        recv[slot, 2 + 2 * c : 4 + 2 * c] = s7[me, 2 * c : 2 * c + 2]
-
-    def await_parts(c):
-        for k in range(NB - 1):
-            part_copy(c, k).wait_recv()
+    def front_copy(half, k):
+        dest = dest_of(k)
+        return pltpu.make_async_remote_copy(
+            src_ref=fsend.at[half, dest], dst_ref=frecv.at[half, slot // 2, slot % 2],
+            send_sem=front_send.at[half, k], recv_sem=front_recv.at[half, k],
+            device_id={"band": dest}, device_id_type=MESH,
+        )
+
+    own_first = range(NB - 1)
+    own_last = [*range(NCOL - 1, NB - 1), *range(NCOL - 1)]
+
+    def start_front(half):
+        for k in own_last:
+            front_copy(half, k).start()
+        frecv[half, slot // 2, slot % 2] = fsend[half, me]
 
     def shift_copy(i):
         return pltpu.make_async_remote_copy(
@@ -178,37 +188,63 @@
         src_ref=hsend, dst_ref=hrecv, send_sem=halo_sem.at[0], recv_sem=halo_sem.at[1],
         device_id={"tm": later}, device_id_type=MESH,
     )
-    edge_copy = pltpu.make_async_remote_copy(
-        src_ref=gsend, dst_ref=grecv, send_sem=halo_sem.at[2], recv_sem=halo_sem.at[3],
-        device_id={"tm": later}, device_id_type=MESH,
-    )
+    edge_copies = [
+        pltpu.make_async_remote_copy(
+            src_ref=gsend.at[e], dst_ref=grecv.at[e],
+            send_sem=halo_sem.at[2 + 2 * e], recv_sem=halo_sem.at[3 + 2 * e],
+            device_id={"tm": later}, device_id_type=MESH,
+        )
+        for e in range(2)
+    ]
     has_next, has_last = t < NT - 1, t > 0
 
-    local_sections(2, 2)
+    s7[...] = local_sections(2)
     pl.semaphore_wait(barrier, NB + NT - 2)
     pl.when(has_next)(halo_copy.start)
     for i in range(1, NB // 2):
         shift_copy(i).start()
-    start_parts(1, range(NB - 1))
+    for k in own_first:
+        back_copy(k).start()
+    recv[slot // 2, slot % 2] = s7[me]
 
     before = jnp.dot(presum[:, 512:], xc[0:512, 256:512], preferred_element_type=F32)
+    for k in range(2):
+        l0[:, k] = before[:, k * 128 : (k + 1) * 128].reshape(32, 8, 128)
+    is_low = iota((32, 8, 128), 1) < 4
+
+    def pack(two_tiles, half):
+        first, second = two_tiles
+        return jnp.where(is_low, *((swap_halves(first), second) if half else (first, swap_halves(second))))
+
+    x = local_sections(0)
+    for half in range(2):
+        fsend[half] = pack((x[:, 0], x[:, 1]), half)
+    start_front(1)
 
     @pl.when(t == 0)
     def _():
-        hrecv[...] = jnp.zeros((2, 128, 128), F32)
-        grecv[...] = jnp.zeros((2, 128, 128), F32)
+        hrecv[...] = jnp.zeros(hrecv.shape, F32)
+        grecv[...] = jnp.zeros(grecv.shape, F32)
 
     pl.when(has_last)(halo_copy.wait_recv)
-    is_low = iota((32, 8, 128), 1) < 4
-
     def spread_edge(packed):
-        return jnp.stack([packed, swap_halves(packed)], axis=1).reshape(32, 8, 128)
-
-    for k in range(2):
-        own = before[:, k * 128 : (k + 1) * 128].reshape(32, 8, 128)
-        l0[:, k] = jnp.where(is_low, spread_edge(hrecv[k].reshape(16, 8, 128)), own)
-    local_sections(0, 2)
-    start_parts(0, [*range(NCOL - 1, NB - 1), *range(NCOL - 1)])
+        return jnp.stack([packed, swap_halves(packed)], axis=1).reshape(-1, 8, 128)
+
+    x = hrecv[...]
+    empty = jnp.zeros((16, 1, 8, 128), F32)
+    for s in range(1, LOCAL + 1):
+        pairs = idx1[s - 1].reshape(16, 2, 8, 128)
+        index = jnp.where(iota((16, 8, 128), 1) < 4, pairs[:, 0], pairs[:, 1])
+        if s in (1, 5):
+            x = jnp.concatenate([x, empty], axis=1)
+        if 2 <= s <= 5:
+            x = major_section(x, index, 2 ** (s - 2))[0]
+        else:
+            x = minor_section(x, index, 4 if s == 1 else 2 ** (7 - s))[0]
+        if s in (3, 7):
+            x = x[:, 1:]
+    fsend[0] = fsend[0] + pack((spread_edge(x[:, 0]), spread_edge(x[:, 1])), 0)
+    start_front(0)
 
     offset, sample = iota((256, 128), 0) - 128, iota((256, 128), 1)
     row = jnp.broadcast_to(par[12:13, :], (8, 128))
@@ -241,22 +277,69 @@
                 delay = take_lanes(row, base + 2**j * quarter + high)
                 idx2[j - 1, low + 2 ** (CROSS - j) * high] = (lane8 - delay) & 127
 
-    await_parts(1)
-    for k in range(2):
-        pairs = recv[:, 4 + k].reshape(16, 2, 8, 128)
-        even, odd = swap_halves(pairs[:, 0]), pairs[:, 1]
-        gsend[k] = jnp.where(iota((16, 8, 128), 1) < 4, even, odd).reshape(128, 128)
-    pl.when(has_next)(edge_copy.start)
-    pl.when(has_last)(edge_copy.wait_recv)
-    for k in range(2):
-        own = swap_halves(recv[:, 4 + k])
-        recv[:, k] = jnp.where(is_low, spread_edge(grecv[k].reshape(16, 8, 128)), own)
-
-    await_parts(0)
-    x = recv[...]
-    for j, keep in ((1, 6), (2, 6), (3, 5), (4, 5), (5, 5)):
-        x = major_section(x, idx2[j - 1], 2 ** (CROSS - j), keep)
-    x = x * (16384.0 ** (-0.5))
+    parity = [column, 1 - column]
+    for e in range(2):
+        for k in range(NCOL - 1) if e == 0 else range(NCOL - 1, NB - 1):
+            back_copy(k).wait_recv()
+        for k in range(2):
+            pairs = recv[:, pl.ds(parity[e], 1), k].reshape(8, 2, 8, 128)
+            gsend[e, k] = jnp.where(iota((8, 8, 128), 1) < 4, swap_halves(pairs[:, 0]), pairs[:, 1])
+        pl.when(has_next)(edge_copies[e].start)
+
+    x = recv[...].reshape(32, 2, 8, 128)
+    for j in range(1, CROSS):
+        x = major_section(x, idx2[j - 1], 2 ** (CROSS - j))[0]
+    tail = x[:, 1:]
+
+    x = jnp.stack([swap_halves(recv[:, :, k].reshape(32, 8, 128)) for k in range(2)], axis=1)
+    x = jnp.where(jnp.broadcast_to(is_low[:, None], x.shape), 0.0, x)
+    aheads = []
+    for j in range(1, CROSS + 1):
+        x, ahead = major_section(x, idx2[j - 1], 2 ** (CROSS - j))
+        aheads.append(ahead)
+        if j == 3:
+            x = x[:, 1:]
+    front = x
+
+    def add_edge():
+        for copy in edge_copies:
+            pl.when(has_last)(copy.wait_recv)
+        x = jnp.stack([grecv[column if f == 0 else 1 - column] for f in range(2)])
+        x = jnp.stack([x[:, 0].reshape(16, 8, 128), x[:, 1].reshape(16, 8, 128)], axis=1)
+        for j in range(1, CROSS + 1):
+            rows = idx2[j - 1].reshape(8, 2, 2, 8, 128)
+            index = [jnp.where(iota((8, 8, 128), 1) < 4, rows[:, 0, f], rows[:, 1, f]) for f in range(2)]
+            index = jnp.concatenate(index, axis=0)
+            if j in (1, CROSS):
+                x = jnp.concatenate([x, jnp.zeros((16, 1, 8, 128), F32)], axis=1)
+            if j == 4:
+                x = minor_section(x, index, 4)[0]
+            else:
+                x = major_section(x, index, 8 if j == CROSS else 2 ** (3 - j))[0]
+            if j == 3:
+                x = x[:, 1:]
+        for k in range(3):
+            parts = [jnp.stack([p, swap_halves(p)], axis=1) for p in (x[:8, k], x[8:, k])]
+            added = jnp.stack(parts, axis=2).reshape(32, 8, 128)
+            extra[:, k] = jnp.where(is_low, added, 0.0)
+
+    is_late = t == NT // 2
+    pl.when(jnp.logical_not(is_late))(add_edge)
+
+    for half in (1, 0):
+        for k in range(NB - 1):
+            front_copy(half, k).wait_recv()
+    low, high = (frecv[half].reshape(32, 8, 128) for half in range(2))
+    first = jnp.where(is_low, low, swap_halves(high))
+    second = jnp.where(is_low, swap_halves(low), high)
+    x = jnp.stack([first, second, recv[:, :, 0].reshape(32, 8, 128)], axis=1)
+    for j in range(1, CROSS + 1):
+        if j == CROSS:
+            x = jnp.concatenate([x, tail], axis=1)
+        x = major_section(x, idx2[j - 1], 2 ** (CROSS - j), aheads[j - 1])[0]
+    pl.when(is_late)(add_edge)
+    x = [x[:, k] + extra[:, k + 1] if k < 2 else x[:, k] for k in range(TILES)]
+    x = jnp.stack([front[:, 0] + extra[:, 0], *x], axis=1) * (16384.0 ** (-0.5))
     for k in range(5):
         t2[k] = x[:, k].reshape(256, 128)
     total = x[:, 1] + x[:, 2] + x[:, 3] + x[:, 4]
@@ -297,15 +380,20 @@
     for k in range(TILES):
         at = pl.ds(k * 128, 256)
         both = jnp.dot(hi[:, at], band[...], preferred_element_type=F32)
-        bc[k] = both + jnp.dot(lo[:, at], band[...], preferred_element_type=F32)
-
-    for c in range(2):
-        for k in range(NB - 1):
-            part_copy(c, k).wait_send()
+        both = both + jnp.dot(lo[:, at], band[...], preferred_element_type=F32)
+        for j in range(NBOX):
+            part = both[:, j * 128 : (j + 1) * 128].reshape(32, 8, 128)
+            bc[k, j] = (part * jnp.broadcast_to(roots[1, j][None], part.shape)).reshape(256, 128)
+
+    for k in range(NB - 1):
+        back_copy(k).wait_send()
+        for half in range(2):
+            front_copy(half, k).wait_send()
     for i in range(1, NB // 2):
         shift_copy(i).wait_send()
     pl.when(has_next)(halo_copy.wait_send)
-    pl.when(has_next)(edge_copy.wait_send)
+    for e in range(2):
+        pl.when(has_next)(edge_copies[e].wait_send)
     for i in range(1, NT):
         stat_copy(i).wait_recv()
     means = [stbuf[i][0:1] for i in range(NT)]
@@ -318,17 +406,17 @@
     row_mean = jnp.broadcast_to(shared[:, 0:1], (256, 128))
     row_scale = jnp.broadcast_to(shared[:, 1:2], (256, 128))
     off = pivot.reshape(256, 128) - row_mean
-    for h in range(4):
-        at = pl.ds(64 * h, 64)
+    for h in range(8):
+        at = pl.ds(32 * h, 32)
         best = [None] * TILES
         for j in range(NBOX):
-            up, down = (jnp.broadcast_to(roots[e, j][None], (8, 8, 128)).reshape(64, 128) for e in range(2))
-            bias = up * off[64 * h : 64 * h + 64]
+            up = jnp.broadcast_to(roots[0, j][None], (4, 8, 128)).reshape(32, 128)
+            bias = up * off[32 * h : 32 * h + 32]
             for k in range(TILES):
-                score = bc[k, at, j * 128 : (j + 1) * 128] * down + bias
+                score = bc[k, j, at] + bias
                 best[k] = score if j == 0 else jnp.maximum(best[k], score)
         for k in range(TILES):
-            t2[k, at] = best[k] * row_scale[64 * h : 64 * h + 64]
+            t2[k, at] = best[k] * row_scale[32 * h : 32 * h + 32]
     unmix(t2, 0, snr_ref)
     for i in range(1, NT):
         stat_copy(i).wait_send()
@@ -347,39 +435,43 @@
     vmem, whole = pltpu.VMEM, pl.BlockSpec(memory_space=pl.ANY)
     in_vmem = pl.BlockSpec(memory_space=pltpu.VMEM)
     out = jax.ShapeDtypeStruct((128, 1024), F32)
-    widths = jnp.pad(boxcar_widths[None], ((12, 3), (0, 128 - NBOX)))
-    params = jnp.pad(shifts, ((0, 4), (0, 0))) + widths
+    params = jnp.pad(shifts, ((0, 4), (0, 0)))
+    params = lax.dynamic_update_slice(params, boxcar_widths[None], (12, 0))
     ded, snr = pl.pallas_call(
         kernel,
         out_shape=(out, out),
-        in_specs=[whole] * 2,
+        in_specs=[whole, in_vmem],
         out_specs=[in_vmem] * 2,
         scratch_shapes=[
             vmem((1024, 512), BF16),
-            vmem((16, 128), I32),
             vmem((4, 1, 128), I32),
             vmem((NB, 4, 1, 128), I32),
             vmem((LOCAL, 32, 8, 128), I32),
             vmem((CROSS, 32, 8, 128), I32),
             vmem((32, 6, 8, 128), F32),
-            vmem((32, TILES, 8, 128), F32),
-            vmem((2, 128, 128), F32),
-            vmem((2, 128, 128), F32),
-            vmem((2, 128, 128), F32),
-            vmem((2, 128, 128), F32),
-            vmem((32, 2 + TILES, 8, 128), F32),
+            vmem((32, 2, 8, 128), F32),
+            vmem((16, 2, 8, 128), F32),
+            vmem((16, 2, 8, 128), F32),
+            vmem((2, 2, 8, 8, 128), F32),
+            vmem((2, 2, 8, 8, 128), F32),
+            vmem((2, 32, 8, 128), F32),
+            vmem((2, 16, 2, 8, 128), F32),
+            vmem((16, 2, 2, 8, 128), F32),
+            vmem((32, 3, 8, 128), F32),
             vmem((5, 256, 128), F32),
             vmem((256, 640), BF16),
             vmem((256, 640), BF16),
-            vmem((TILES, 256, 1024), F32),
+            vmem((TILES, NBOX, 256, 128), F32),
             vmem((256, 1024), BF16),
             vmem((2, NBOX, 8, 128), F32),
             vmem((8, 256), F32),
             vmem((NT, 8, 256), F32),
-            dma((3,)),
+            dma((2,)),
             dma((NB // 2,)),
             dma((NB // 2,)),
-            dma((4,)),
+            dma((6,)),
+            dma((NB - 1,)),
+            dma((NB - 1,)),
             dma((2, NB - 1)),
             dma((2, NB - 1)),
             dma((NT,)),

time: 37.9 us -> 36.8 us (0.971)
  Pallas kernels: 35.8 us -> 35 us
  other arithmetic: 0.7 us -> 0 us
    pallas_call x1, Pallas kernels: 34.8 us -> 34 us  [body(): pl.pallas_call(kernel, out_shape=(out, out), in_specs=[whole, in_vmem], o...]
    pad x0 -> x1, local copies, waits for them, and re-layouts: none -> 0.71 us  [body(): params = jnp.pad(shifts, ((0, 4), (0, 0)))]
    add x1 -> x0, other arithmetic: 0.7 us -> none  [body(): params = jnp.pad(shifts, ((0, 4), (0, 0))) + widths]
    unnamed x2, local copies, waits for them, and re-layouts: 0.65 us -> 0.01 us
where the time goes in v1:
time: 36.8 us; the launch traced here: 36.6 us
  Pallas kernels  35 us (95%)
  local copies, waits for them, and re-layouts  0.85 us (2%)
  between operations  0.82 us (2%)
    pallas_call x1, Pallas kernels, body(): pl.pallas_call(kernel, out_shape=(out, out), in_specs=[whole, in_vmem], o...  34 us
    pallas_call x1, Pallas kernels, body(): pl.pallas_call(store, out_shape=(out, out), in_specs=[in_vmem] * 2, out_s...  0.99 us

profile of v1, /device:TPU:1, one launch (start us, length us, event | category | flops | bytes accessed | tf_op | source)
XLA Modules:
  0.0 36.6 jit_solution(12436733916023442117)
XLA Ops:
  0.6 0.0 copy-start
  0.6 0.7 %pad.4 = s32[16,128]{1,0:T(8,128)S(1)} pad(s32[12,128]{1,0:T(8,128)} %param.4, s32[]{:T(128)} %constant.0.clone.1), padding=0_4x0_0 | pad | bytes 14340 | tf_op jit(solution)/shard_map/jit(_pad)/pad | solution.py:438
  1.3 0.0 copy-done
  1.4 0.1 dynamic_update_slice.3.par
  1.5 34.0 %shard_map.50 = (f32[128,1024]{1,0:T(8,128)S(1)}, f32[128,1024]{1,0:T(8,128)S(1)}) custom-call(bf16[512,1024]{1,0:T(8,128)(2,1)} %x_hbm.1, s32[16,128]{1,0:T(8,128)S(1)} %dynamic_update_slice.3.par), custom_call_target="tpu_custom_call" | custom-call | tf_op jit(solution)/shard_map/pallas_call | solution.py:440
  35.5 1.0 %shard_map.51 = (f32[128,1024]{1,0:T(8,128)}, f32[128,1024]{1,0:T(8,128)}) custom-call(f32[128,1024]{1,0:T(8,128)S(1)} %get-tuple-element.4.a, f32[128,1024]{1,0:T(8,128)S(1)} %get-tuple-element.5.b), custom_call_target="tpu_custom_call" | custom-call | tf_op jit(solution)/shard_map/pallas_call | solution.py:484
Async XLA Ops:
  0.6 0.7 %copy-start = (s32[8]{0:T(128)S(1)}, s32[8]{0:T(128)}, u32[]{:S(2)}) copy-start(s32[8]{0:T(128)} %param.5) | copy-start | bytes 100

commit v2 on v1

v2 whole, which is shorter than its diff:
```python
import jax
import jax.numpy as jnp
from jax import lax
from jax.experimental import pallas as pl
from jax.experimental.pallas import tpu as pltpu
from jax.sharding import PartitionSpec as P

MESH = pl.DeviceIdType.MESH
F32, BF16, I32 = jnp.float32, jnp.bfloat16, jnp.int32
NB, NT = 32, 8
NBOX = 8
NCOL = 16
LOCAL, CROSS = 7, 5
TILES = 4
SAMPLES = 8192

_ROWS = lax.GatherDimensionNumbers(
    offset_dims=(),
    collapsed_slice_dims=(1,),
    start_index_map=(1,),
    operand_batching_dims=(0,),
    start_indices_batching_dims=(0,),
)


def iota(shape, dim):
    return lax.broadcasted_iota(I32, shape, dim)


def take_lanes(x, index):
    return lax.gather(
        x, index[..., None], _ROWS, (1, 1), mode=lax.GatherScatterMode.PROMISE_IN_BOUNDS
    )


def rev5(v):
    out = 0
    for k in range(5):
        out = out + (v // 2**k) % 2 * 2 ** (4 - k)
    return out


OFFSETS = sorted(
    [(dx, dz, dc) for dx in range(2) for dz in range(8) for dc in range(2)][1:],
    key=lambda o: (o[0], -min(o[1], 8 - o[1])),
)


def delay_add(firsts, seconds, index, ahead=None):
    spread = jnp.broadcast_to(index[:, None], firsts.shape).reshape(-1, 128)
    turned = take_lanes(seconds.reshape(-1, 128), spread).reshape(firsts.shape)
    last = turned[:, -1:]
    if ahead is not None:
        before = jnp.concatenate([ahead, turned[:, :-1]], axis=1)
    elif firsts.shape[1] == 1:
        return firsts + turned, last
    else:
        before = jnp.concatenate([turned[:, :1], turned[:, :-1]], axis=1)
    wraps = jnp.broadcast_to((index > iota(index.shape, 2))[:, None], firsts.shape)
    return firsts + jnp.where(wraps, before, turned), last


def major_section(x, index, apart, ahead=None):
    rows, tiles = x.shape[:2]
    shape = (rows // (2 * apart), 2, apart, tiles, 8, 128)
    pairs = x.reshape(shape)
    both = [jnp.broadcast_to(pairs[:, e : e + 1], shape).reshape(x.shape) for e in (0, 1)]
    return delay_add(*both, index, ahead)


def folded_section(x, index, apart, grow):
    rows, tiles = x.shape[:2]
    shape = (rows // (2 * apart), 2, apart, tiles, 8, 128)
    pairs = x.reshape(shape)
    firsts, seconds = (jnp.broadcast_to(pairs[:, e : e + 1], shape).reshape(x.shape) for e in (0, 1))
    spread = jnp.broadcast_to(index[:, None], x.shape).reshape(-1, 128)
    turned = take_lanes(seconds.reshape(-1, 128), spread).reshape(x.shape)
    swapped = swap_halves(turned)
    is_low, wraps = iota(index.shape, 1) < 4, index > iota(index.shape, 2)
    empty, outs = jnp.zeros(index.shape, F32), []
    for v in range(tiles + grow):
        before = jnp.where(is_low, swapped[:, v - 1] if v else empty, swapped[:, v] if v < tiles else empty)
        if v < tiles:
            outs.append(firsts[:, v] + jnp.where(wraps, before, turned[:, v]))
        else:
            outs.append(jnp.where(wraps, before, 0.0))
    return jnp.stack(outs, axis=1)


def minor_section(x, index, apart):
    flat = x.reshape(-1, 8, 128)
    is_set = iota(flat.shape, 1) // apart % 2 == 1
    firsts = jnp.where(is_set, pltpu.roll(flat, apart, 1), flat)
    seconds = jnp.where(is_set, flat, pltpu.roll(flat, 8 - apart, 1))
    return delay_add(firsts.reshape(x.shape), seconds.reshape(x.shape), index)


def swap_halves(x):
    return pltpu.roll(x.reshape(-1, 8, 128), 4, 1).reshape(x.shape)


def kernel(
    x_hbm, par, ded_ref, snr_ref,
    xc, shsend, shbuf, idx1, idx2, l0, s7, hsend, hrecv, grecv, fsend, frecv,
    recv, extra, t2, hi, lo, bc, band, roots, stsend, stbuf,
    local_sem, shs_sem, shr_sem, halo_sem, main_send, main_recv, front_send, front_recv, st_send, st_recv,
):
    me, t = lax.axis_index("band"), lax.axis_index("tm")
    copies_x = [
        pltpu.make_async_copy(x_hbm.at[pl.ds(128 * i, 128)], xc.at[pl.ds(128 * i, 128)], local_sem.at[i])
        for i in range(4)
    ]
    for copy in copies_x:
        copy.start()

    barrier = pltpu.get_barrier_semaphore()
    for i in range(1, NB):
        pl.semaphore_signal(barrier, inc=1, device_id={"band": lax.rem(me + i, NB)}, device_id_type=MESH)
    for i in range(1, NT):
        pl.semaphore_signal(barrier, inc=1, device_id={"tm": lax.rem(t + i, NT)}, device_id_type=MESH)

    column, place = me // NCOL, me % NCOL
    z, core = place // 2, place % 2
    later = lax.rem(t + 1, NT)
    slot = rev5(me)
    sub8, lane8 = iota((8, 128), 0), iota((8, 128), 1)

    ones = jnp.ones((128, 128), BF16)
    for s in range(1, LOCAL + 1):
        row = jnp.broadcast_to(par[s - 1 : s, :].astype(F32), (8, 128))
        if s <= 5:
            base = sub8 // 2 % 2 * 32 + sub8 % 2 * 64
        else:
            base = sub8 // 2 % 2 * (1, 2)[s - 6] + sub8 % 2 * (64, 1)[s - 6]
        picks = []
        for m in range(32):
            turned = int(f"{m:05b}"[::-1], 2)
            if s <= 5:
                turned = (turned >> (5 - s)) + (m >> s << s)
            else:
                turned = turned << (s - 5)
            picks.append(jnp.where(lane8 - base == turned, row, 0.0))
        picks = jnp.stack(picks).reshape(256, 128).astype(BF16)
        delay = jnp.dot(picks, ones, preferred_element_type=F32).astype(I32)
        idx1[s - 1] = ((iota((256, 128), 1) - delay) & 127).reshape(32, 8, 128)
    for j in range(CROSS - 1):
        shsend[j] = par[LOCAL + j : LOCAL + j + 1, :]
        shbuf[me, j] = par[LOCAL + j : LOCAL + j + 1, :]

    is_low = iota((32, 8, 128), 1) < 4
    i = iota((128, 512), 0)
    group = i // 4 + 32 * (i // 2 % 2) + 64 * (i % 2)
    presum = jnp.where(iota((128, 512), 1) // 4 == group, 1.0, 0.0).astype(BF16)
    level = 0.0
    for i in range(2):
        copies_x[2 * i].wait()
        copies_x[2 * i + 1].wait()
        at = pl.ds(256 * i, 256)
        level = level + jnp.dot(presum[:, 256 * i : 256 * i + 256], xc[at], preferred_element_type=F32)
    for k in range(TILES):
        low, high = (level[:, c * 128 : c * 128 + 128].reshape(16, 8, 128) for c in (k, k + 4))
        if k >= 2:
            hsend[:, k - 2] = high
        low, high = (jnp.stack([p, swap_halves(p)], axis=1).reshape(32, 8, 128) for p in (low, swap_halves(high)))
        l0[:, 2 + k] = jnp.where(is_low, low, high)
        if k >= 2:
            l0[:, k - 2] = jnp.where(is_low, 0.0, swap_halves(low))

    def pack(two_tiles, half):
        first, second = two_tiles
        return jnp.where(is_low, *((swap_halves(first), second) if half else (first, swap_halves(second))))

    def dest_of(k):
        dx, dz, dc = OFFSETS[k]
        return (column + dx) % 2 * NCOL + (z + dz) % 8 * 2 + (core + dc) % 2

    def main_copy(part, k):
        dest, which = dest_of(k), (pl.ds(0, 1), pl.ds(1, 2))[part]
        return pltpu.make_async_remote_copy(
            src_ref=s7.at[dest, which], dst_ref=recv.at[slot // 2, slot % 2, which],
            send_sem=main_send.at[part, k], recv_sem=main_recv.at[part, k],
            device_id={"band": dest}, device_id_type=MESH,
        )

    def front_copy(k):
        dest = dest_of(k)
        return pltpu.make_async_remote_copy(
            src_ref=fsend.at[dest], dst_ref=frecv.at[slot // 2, slot % 2],
            send_sem=front_send.at[k], recv_sem=front_recv.at[k],
            device_id={"band": dest}, device_id_type=MESH,
        )

    own, other = range(NCOL - 1), range(NCOL - 1, NB - 1)
    edges_first = t % 4 == 3

    def start_all(copies):
        for copy in copies:
            copy.start()

    def shift_copy(i):
        needed = pl.ds(0, (i & -i).bit_length())
        return pltpu.make_async_remote_copy(
            src_ref=shsend.at[needed], dst_ref=shbuf.at[me, needed], send_sem=shs_sem.at[i], recv_sem=shr_sem.at[i],
            device_id={"band": lax.rem(me + 2 * i, NB)}, device_id_type=MESH,
        )

    halo_copy = pltpu.make_async_remote_copy(
        src_ref=hsend, dst_ref=hrecv, send_sem=halo_sem.at[0], recv_sem=halo_sem.at[1],
        device_id={"tm": later}, device_id_type=MESH,
    )
    edge_copies = [
        pltpu.make_async_remote_copy(
            src_ref=recv.at[:, column if e == 0 else 1 - column, 0], dst_ref=grecv.at[e],
            send_sem=halo_sem.at[2 + 2 * e], recv_sem=halo_sem.at[3 + 2 * e],
            device_id={"tm": later}, device_id_type=MESH,
        )
        for e in range(2)
    ]
    has_next, has_last = t < NT - 1, t > 0

    def local_sections(first):
        x = l0[:, first : first + 4]
        for s in range(1, LOCAL + 1):
            if s <= 5:
                x = major_section(x, idx1[s - 1], 2 ** (s - 1))[0]
            else:
                x = minor_section(x, idx1[s - 1], 2 ** (7 - s))[0]
            if s in (3, 7):
                x = x[:, 1:]
        return x[:, 0], x[:, 1]

    tiles = local_sections(2)
    s7[:, 0] = pack(tiles, 1)
    s7[:, 1] = pack(tiles, 0)
    pl.semaphore_wait(barrier, NB + NT - 2)
    pl.when(has_next)(halo_copy.start)
    for i in range(1, NB // 2):
        shift_copy(i).start()
    start_all(main_copy(0, k) for k in [*own, *other])
    tiles = local_sections(0)
    s7[:, 2] = pack(tiles, 1)
    fsend[...] = pack(tiles, 0)
    pl.when(jnp.logical_not(edges_first))(lambda: start_all(main_copy(1, k) for k in other))
    start_all(main_copy(1, k) for k in own)
    pl.when(edges_first)(lambda: start_all(main_copy(1, k) for k in other))
    recv[slot // 2, slot % 2] = s7[me]

    offset, sample = iota((256, 128), 0) - 128, iota((256, 128), 1)
    row = jnp.broadcast_to(par[12:13, :], (8, 128))
    for j in range(NBOX):
        width = take_lanes(row, jnp.full((8, 128), j, I32))
        root = jnp.sqrt(width.astype(F32))
        roots[0, j] = root
        roots[1, j] = 1.0 / root
        width = jnp.broadcast_to(width[None], (32, 8, 128)).reshape(256, 128)
        inside = (offset <= sample) & (offset > sample - width)
        band[:, j * 128 : (j + 1) * 128] = jnp.where(inside, 1.0, 0.0).astype(BF16)

    @pl.when(t == 0)
    def _():
        hrecv[...] = jnp.zeros(hrecv.shape, F32)
        grecv[...] = jnp.zeros(grecv.shape, F32)

    pl.when(has_last)(halo_copy.wait_recv)
    def spread_edge(packed):
        return jnp.stack([packed, swap_halves(packed)], axis=1).reshape(-1, 8, 128)

    x = hrecv[...]
    empty = jnp.zeros((16, 1, 8, 128), F32)
    for s in range(1, LOCAL + 1):
        pairs = idx1[s - 1].reshape(16, 2, 8, 128)
        index = jnp.where(iota((16, 8, 128), 1) < 4, pairs[:, 0], pairs[:, 1])
        if s in (1, 5):
            x = jnp.concatenate([x, empty], axis=1)
        if 2 <= s <= 5:
            x = major_section(x, index, 2 ** (s - 2))[0]
        else:
            x = minor_section(x, index, 4 if s == 1 else 2 ** (7 - s))[0]
        if s in (3, 7):
            x = x[:, 1:]
    fsend[...] = fsend[...] + pack((spread_edge(x[:, 0]), spread_edge(x[:, 1])), 0)
    start_all(front_copy(k) for k in [*other, *own])
    frecv[slot // 2, slot % 2] = fsend[me]

    for e in range(2):
        for k in other if e else own:
            main_copy(0, k).wait_recv()
        pl.when(has_next)(edge_copies[e].start)

    for i in range(1, NB // 2):
        shift_copy(i).wait_recv()
    quarter = sub8 % 4
    for j in range(1, CROSS + 1):
        base = 0
        for bit in range(j, CROSS):
            base = base + me // 2**bit % 2 * 2 ** (6 - bit + j)
        for low in range(2 ** (CROSS - j)):
            if j < CROSS:
                source = me % 2**j
                for bit in range(j, CROSS):
                    source = source + 2**bit * ((low >> (4 - bit)) & 1)
                row = shbuf[source, j - 1]
            else:
                row = par[LOCAL + j - 1 : LOCAL + j, :]
            row = jnp.broadcast_to(row, (8, 128))
            for high in range(2**j):
                delay = take_lanes(row, base + 2**j * quarter + high)
                idx2[j - 1, low + 2 ** (CROSS - j) * high] = (lane8 - delay) & 127

    def add_edge():
        for copy in edge_copies:
            pl.when(has_last)(copy.wait_recv)
        x = jnp.stack([grecv[column if f == 0 else 1 - column] for f in range(2)], axis=1).reshape(32, 1, 8, 128)
        for j in range(1, CROSS + 1):
            x = folded_section(x, idx2[j - 1], 2 ** (CROSS - j), j == 1)
        for k, part in enumerate([swap_halves(x[:, 0]), x[:, 1], swap_halves(x[:, 1])]):
            extra[:, k] = part

    is_late = t == NT // 2
    pl.when(jnp.logical_not(is_late))(add_edge)

    for k in [*other, *own]:
        main_copy(1, k).wait_recv()

    def unpack(low, high):
        return jnp.where(is_low, low, swap_halves(high)), jnp.where(is_low, swap_halves(low), high)

    back = unpack(recv[:, :, 1].reshape(32, 8, 128), recv[:, :, 0].reshape(32, 8, 128))
    x = swap_halves(jnp.stack(back, axis=1))
    x = jnp.where(jnp.broadcast_to(is_low[:, None], x.shape), 0.0, x)
    aheads = []
    for j in range(1, CROSS + 1):
        x, ahead = major_section(x, idx2[j - 1], 2 ** (CROSS - j))
        aheads.append(ahead)
        if j == 3:
            x = x[:, 1:]
    front = x

    high = recv[:, :, 2].reshape(32, 8, 128)
    x = jnp.stack([jnp.where(is_low, 0.0, swap_halves(high)), jnp.where(is_low, 0.0, high), *back], axis=1)
    for j in range(1, CROSS + 1):
        x = major_section(x, idx2[j - 1], 2 ** (CROSS - j), aheads[j - 1])[0]
    norm = 16384.0 ** (-0.5)
    x = jnp.concatenate([front, x], axis=1) * norm
    total = x[:, 1] + x[:, 2] + x[:, 3] + x[:, 4]
    total = jnp.sum(jnp.where(is_low, 0.0, total), axis=2, keepdims=True)
    pivot = jnp.broadcast_to(total * (1.0 / 512), (32, 8, 128))
    pivot = pivot + swap_halves(pivot)

    for k in range(NB - 1):
        front_copy(k).wait_recv()
    y = frecv[...].reshape(32, 1, 8, 128)
    for j in range(1, CROSS + 1):
        y = folded_section(y, idx2[j - 1], 2 ** (CROSS - j), j == 1)
    pl.when(is_late)(add_edge)
    added = [extra[:, 0], extra[:, 1] + y[:, 0], extra[:, 2] + swap_halves(y[:, 0]), y[:, 1], swap_halves(y[:, 1])]
    x = x + jnp.stack([jnp.where(is_low, part, 0.0) * norm for part in added], axis=1)
    centred = x - jnp.broadcast_to(pivot[:, None], x.shape)
    sums, squares = centred[:, 1], centred[:, 1] * centred[:, 1]
    for k in range(2, 5):
        sums = sums + centred[:, k]
        squares = squares + centred[:, k] * centred[:, k]
    sums = jnp.broadcast_to(jnp.sum(sums + swap_halves(sums), axis=2, keepdims=True), (32, 8, 128))
    squares = jnp.broadcast_to(jnp.sum(squares + swap_halves(squares), axis=2, keepdims=True), (32, 8, 128))
    squares = squares - sums * sums * (1.0 / 1024)
    sums = pivot + sums * (1.0 / 1024)
    packed = jnp.where(iota((32, 8, 128), 2) == 0, sums, squares)
    mine = jnp.transpose(packed.reshape(256, 128))[0:2]
    stsend[...] = mine
    stbuf[t] = mine

    def stat_copy(i):
        return pltpu.make_async_remote_copy(
            src_ref=stsend, dst_ref=stbuf.at[t], send_sem=st_send.at[i], recv_sem=st_recv.at[i],
            device_id={"tm": lax.rem(t + i, NT)}, device_id_type=MESH,
        )

    for i in range(1, NT):
        stat_copy(i).start()

    def unmix(source, first, out):
        for k in range(TILES):
            for s in range(8):
                for b in range(4):
                    rows = source[first + k, pl.ds(b * 64 + s, 8, stride=8), :]
                    out[pl.ds(s % 4 * 32 + b * 8, 8), pl.ds(s // 4 * 512 + k * 128, 128)] = rows

    for k in range(5):
        t2[k] = x[:, k].reshape(256, 128)
        part = centred[:, k].reshape(256, 128)
        high = part.astype(BF16)
        hi[:, k * 128 : (k + 1) * 128] = high
        lo[:, k * 128 : (k + 1) * 128] = (part - high.astype(F32)).astype(BF16)
    unmix(t2, 1, ded_ref)
    for k in range(TILES):
        at = pl.ds(k * 128, 256)
        both = jnp.dot(hi[:, at], band[...], preferred_element_type=F32)
        both = both + jnp.dot(lo[:, at], band[...], preferred_element_type=F32)
        for j in range(NBOX):
            part = both[:, j * 128 : (j + 1) * 128].reshape(32, 8, 128)
            bc[k, j] = (part * jnp.broadcast_to(roots[1, j][None], part.shape)).reshape(256, 128)

    for k in range(NB - 1):
        main_copy(0, k).wait_send()
        main_copy(1, k).wait_send()
        front_copy(k).wait_send()
    for i in range(1, NB // 2):
        shift_copy(i).wait_send()
    pl.when(has_next)(halo_copy.wait_send)
    for e in range(2):
        pl.when(has_next)(edge_copies[e].wait_send)
    for i in range(1, NT):
        stat_copy(i).wait_recv()
    means = [stbuf[i][0:1] for i in range(NT)]
    mean = sum(means) * (1.0 / NT)
    centred = [stbuf[i][1:2] + 1024.0 * ((m - mean) * (m - mean)) for i, m in enumerate(means)]
    scale = 1.0 / jnp.sqrt(sum(centred) * (1.0 / SAMPLES) + 1e-6)
    row_mean = jnp.transpose(jnp.broadcast_to(mean, (128, 256)))
    row_scale = jnp.transpose(jnp.broadcast_to(scale, (128, 256)))
    off = pivot.reshape(256, 128) - row_mean
    for h in range(8):
        at = pl.ds(32 * h, 32)
        best = [None] * TILES
        for j in range(NBOX):
            up = jnp.broadcast_to(roots[0, j][None], (4, 8, 128)).reshape(32, 128)
            bias = up * off[32 * h : 32 * h + 32]
            for k in range(TILES):
                score = bc[k, j, at] + bias
                best[k] = score if j == 0 else jnp.maximum(best[k], score)
        for k in range(TILES):
            t2[k, at] = best[k] * row_scale[32 * h : 32 * h + 32]
    unmix(t2, 0, snr_ref)
    for i in range(1, NT):
        stat_copy(i).wait_send()


def store(a, b, a_hbm, b_hbm, sem):
    copies = []
    for i, (source, target) in enumerate(((a, a_hbm), (b, b_hbm))):
        for j in range(4):
            at = pl.ds(32 * j, 32)
            copies.append(pltpu.make_async_copy(source.at[at], target.at[at], sem.at[i, j]))
    for copy in copies:
        copy.start()
    for copy in copies:
        copy.wait()


def body(intensity, shifts, boxcar_widths):
    dma = pltpu.SemaphoreType.DMA
    vmem, whole = pltpu.VMEM, pl.BlockSpec(memory_space=pl.ANY)
    in_vmem = pl.BlockSpec(memory_space=pltpu.VMEM)
    out = jax.ShapeDtypeStruct((128, 1024), F32)
    params = jnp.pad(shifts, ((0, 4), (0, 0)))
    params = lax.dynamic_update_slice(params, boxcar_widths[None], (12, 0))
    ded, snr = pl.pallas_call(
        kernel,
        out_shape=(out, out),
        in_specs=[whole, in_vmem],
        out_specs=[in_vmem] * 2,
        scratch_shapes=[
            vmem((512, 1024), BF16),
            vmem((4, 1, 128), I32),
            vmem((NB, 4, 1, 128), I32),
            vmem((LOCAL, 32, 8, 128), I32),
            vmem((CROSS, 32, 8, 128), I32),
            vmem((32, 6, 8, 128), F32),
            vmem((32, 3, 8, 128), F32),
            vmem((16, 2, 8, 128), F32),
            vmem((16, 2, 8, 128), F32),
            vmem((2, 16, 8, 128), F32),
            vmem((32, 8, 128), F32),
            vmem((16, 2, 8, 128), F32),
            vmem((16, 2, 3, 8, 128), F32),
            vmem((32, 3, 8, 128), F32),
            vmem((5, 256, 128), F32),
            vmem((256, 640), BF16),
            vmem((256, 640), BF16),
            vmem((TILES, NBOX, 256, 128), F32),
            vmem((256, 1024), BF16),
            vmem((2, NBOX, 8, 128), F32),
            vmem((2, 256), F32),
            vmem((NT, 2, 256), F32),
            dma((4,)),
            dma((NB // 2,)),
            dma((NB // 2,)),
            dma((6,)),
            dma((2, NB - 1)),
            dma((2, NB - 1)),
            dma((NB - 1,)),
            dma((NB - 1,)),
            dma((NT,)),
            dma((NT,)),
        ],
        compiler_params=pltpu.CompilerParams(
            collective_id=0, has_side_effects=True, vmem_limit_bytes=52 * 2**20
        ),
    )(intensity, params)
    return pl.pallas_call(
        store,
        out_shape=(out, out),
        in_specs=[in_vmem] * 2,
        out_specs=[whole] * 2,
        scratch_shapes=[dma((2, 4))],
        compiler_params=pltpu.CompilerParams(vmem_limit_bytes=52 * 2**20),
    )(ded, snr)


def solution(mesh):
    assert mesh.shape["band"] == NB and mesh.shape["tm"] == NT
    in_specs = (P("band", "tm"), P(None, "band"), P())
    out_specs = (P("band", "tm"), P("band", "tm"))
    return jax.shard_map(body, mesh=mesh, in_specs=in_specs, out_specs=out_specs, check_vma=False)
```

time: 36.8 us -> 36.3 us (0.986)
  Pallas kernels: 35 us -> 34.5 us
    pallas_call x1, Pallas kernels: 34 us -> 33.4 us  [body(): pl.pallas_call(kernel, out_shape=(out, out), in_specs=[whole, in_vmem], o...]
where the time goes in v2:
time: 36.3 us; the launch traced here: 36.1 us
  Pallas kernels  34.5 us (95%)
  local copies, waits for them, and re-layouts  0.85 us (2%)
  between operations  0.82 us (2%)
    pallas_call x1, Pallas kernels, body(): pl.pallas_call(kernel, out_shape=(out, out), in_specs=[whole, in_vmem], o...  33.4 us
    pallas_call x1, Pallas kernels, body(): pl.pallas_call(store, out_shape=(out, out), in_specs=[in_vmem] * 2, out_s...  1.03 us

profile of v2, /device:TPU:1, one launch (start us, length us, event | category | flops | bytes accessed | tf_op | source)
XLA Modules:
  0.0 36.1 jit_solution(16403090001274609090)
XLA Ops:
  0.6 0.0 copy-start
  0.6 0.7 %pad.4 = s32[16,128]{1,0:T(8,128)S(1)} pad(s32[12,128]{1,0:T(8,128)} %param.4, s32[]{:T(128)} %constant.0.clone.1), padding=0_4x0_0 | pad | bytes 14340 | tf_op jit(solution)/shard_map/jit(_pad)/pad | solution.py:454
  1.3 0.0 copy-done
  1.4 0.1 dynamic_update_slice.3.par
  1.5 33.4 %shard_map.50 = (f32[128,1024]{1,0:T(8,128)S(1)}, f32[128,1024]{1,0:T(8,128)S(1)}) custom-call(bf16[512,1024]{1,0:T(8,128)(2,1)} %x_hbm.1, s32[16,128]{1,0:T(8,128)S(1)} %dynamic_update_slice.3.par), custom_call_target="tpu_custom_call" | custom-call | tf_op jit(solution)/shard_map/pallas_call | solution.py:456
  34.9 1.0 %shard_map.51 = (f32[128,1024]{1,0:T(8,128)}, f32[128,1024]{1,0:T(8,128)}) custom-call(f32[128,1024]{1,0:T(8,128)S(1)} %get-tuple-element.4.a, f32[128,1024]{1,0:T(8,128)S(1)} %get-tuple-element.5.b), custom_call_target="tpu_custom_call" | custom-call | tf_op jit(solution)/shard_map/pallas_call | solution.py:499
Async XLA Ops:
  0.6 0.7 %copy-start = (s32[8]{0:T(128)S(1)}, s32[8]{0:T(128)}, u32[]{:S(2)}) copy-start(s32[8]{0:T(128)} %param.5) | copy-start | bytes 100

commit v3 on v2

--- a/solution.py
+++ b/solution.py
@@ -46,26 +46,25 @@
 )
 
 
-def delay_add(firsts, seconds, index, ahead=None):
-    spread = jnp.broadcast_to(index[:, None], firsts.shape).reshape(-1, 128)
-    turned = take_lanes(seconds.reshape(-1, 128), spread).reshape(firsts.shape)
-    last = turned[:, -1:]
-    if ahead is not None:
-        before = jnp.concatenate([ahead, turned[:, :-1]], axis=1)
-    elif firsts.shape[1] == 1:
-        return firsts + turned, last
-    else:
-        before = jnp.concatenate([turned[:, :1], turned[:, :-1]], axis=1)
-    wraps = jnp.broadcast_to((index > iota(index.shape, 2))[:, None], firsts.shape)
-    return firsts + jnp.where(wraps, before, turned), last
-
-
-def major_section(x, index, apart, ahead=None):
+def delay_add(firsts, seconds, index, keep):
+    rows, tiles = firsts.shape[:2]
+    shape = (rows, keep, 8, 128)
+    before = seconds[:, tiles - keep - 1 : tiles - 1] if keep < tiles else seconds
+    if keep == tiles > 1:
+        before = jnp.concatenate([seconds[:, :1], seconds[:, :-1]], axis=1)
+    lane = iota(index.shape, 2)
+    wraps = jnp.broadcast_to((((lane + lane - index) & 127) < lane)[:, None], shape)
+    merged = jnp.where(wraps, before, seconds[:, tiles - keep :])
+    spread = jnp.broadcast_to(index[:, None], shape).reshape(-1, 128)
+    return firsts[:, tiles - keep :] + take_lanes(merged.reshape(-1, 128), spread).reshape(shape)
+
+
+def major_section(x, index, apart, keep):
     rows, tiles = x.shape[:2]
     shape = (rows // (2 * apart), 2, apart, tiles, 8, 128)
     pairs = x.reshape(shape)
     both = [jnp.broadcast_to(pairs[:, e : e + 1], shape).reshape(x.shape) for e in (0, 1)]
-    return delay_add(*both, index, ahead)
+    return delay_add(*both, index, keep)
 
 
 def folded_section(x, index, apart, grow):
@@ -87,12 +86,12 @@
     return jnp.stack(outs, axis=1)
 
 
-def minor_section(x, index, apart):
+def minor_section(x, index, apart, keep):
     flat = x.reshape(-1, 8, 128)
     is_set = iota(flat.shape, 1) // apart % 2 == 1
     firsts = jnp.where(is_set, pltpu.roll(flat, apart, 1), flat)
     seconds = jnp.where(is_set, flat, pltpu.roll(flat, 8 - apart, 1))
-    return delay_add(firsts.reshape(x.shape), seconds.reshape(x.shape), index)
+    return delay_add(firsts.reshape(x.shape), seconds.reshape(x.shape), index, keep)
 
 
 def swap_halves(x):
@@ -102,7 +101,7 @@
 def kernel(
     x_hbm, par, ded_ref, snr_ref,
     xc, shsend, shbuf, idx1, idx2, l0, s7, hsend, hrecv, grecv, fsend, frecv,
-    recv, extra, t2, hi, lo, bc, band, roots, stsend, stbuf,
+    recv, t2, hi, lo, bc, band, roots, stsend, stbuf,
     local_sem, shs_sem, shr_sem, halo_sem, main_send, main_recv, front_send, front_recv, st_send, st_recv,
 ):
     me, t = lax.axis_index("band"), lax.axis_index("tm")
@@ -114,13 +113,20 @@
         copy.start()
 
     barrier = pltpu.get_barrier_semaphore()
-    for i in range(1, NB):
-        pl.semaphore_signal(barrier, inc=1, device_id={"band": lax.rem(me + i, NB)}, device_id_type=MESH)
+    column, place = me // NCOL, me % NCOL
+    z, core = place // 2, place % 2
+
+    def dest_of(k):
+        dx, dz, dc = OFFSETS[k]
+        return (column + dx) % 2 * NCOL + (z + dz) % 8 * 2 + (core + dc) % 2
+
+    own, other = range(NCOL - 1), range(NCOL - 1, NB - 1)
+    for k in other:
+        pl.semaphore_signal(barrier, inc=1, device_id={"band": dest_of(k)}, device_id_type=MESH)
     for i in range(1, NT):
         pl.semaphore_signal(barrier, inc=1, device_id={"tm": lax.rem(t + i, NT)}, device_id_type=MESH)
-
-    column, place = me // NCOL, me % NCOL
-    z, core = place // 2, place % 2
+    for k in own:
+        pl.semaphore_signal(barrier, inc=1, device_id={"band": dest_of(k)}, device_id_type=MESH)
     later = lax.rem(t + 1, NT)
     slot = rev5(me)
     sub8, lane8 = iota((8, 128), 0), iota((8, 128), 1)
@@ -170,10 +176,6 @@
         first, second = two_tiles
         return jnp.where(is_low, *((swap_halves(first), second) if half else (first, swap_halves(second))))
 
-    def dest_of(k):
-        dx, dz, dc = OFFSETS[k]
-        return (column + dx) % 2 * NCOL + (z + dz) % 8 * 2 + (core + dc) % 2
-
     def main_copy(part, k):
         dest, which = dest_of(k), (pl.ds(0, 1), pl.ds(1, 2))[part]
         return pltpu.make_async_remote_copy(
@@ -190,7 +192,6 @@
             device_id={"band": dest}, device_id_type=MESH,
         )
 
-    own, other = range(NCOL - 1), range(NCOL - 1, NB - 1)
     edges_first = t % 4 == 3
 
     def start_all(copies):
@@ -221,12 +222,11 @@
     def local_sections(first):
         x = l0[:, first : first + 4]
         for s in range(1, LOCAL + 1):
+            keep = x.shape[1] - (s in (3, 7))
             if s <= 5:
-                x = major_section(x, idx1[s - 1], 2 ** (s - 1))[0]
+                x = major_section(x, idx1[s - 1], 2 ** (s - 1), keep)
             else:
-                x = minor_section(x, idx1[s - 1], 2 ** (7 - s))[0]
-            if s in (3, 7):
-                x = x[:, 1:]
+                x = minor_section(x, idx1[s - 1], 2 ** (7 - s), keep)
         return x[:, 0], x[:, 1]
 
     tiles = local_sections(2)
@@ -272,12 +272,11 @@
         index = jnp.where(iota((16, 8, 128), 1) < 4, pairs[:, 0], pairs[:, 1])
         if s in (1, 5):
             x = jnp.concatenate([x, empty], axis=1)
+        keep = x.shape[1] - (s in (3, 7))
         if 2 <= s <= 5:
-            x = major_section(x, index, 2 ** (s - 2))[0]
+            x = major_section(x, index, 2 ** (s - 2), keep)
         else:
-            x = minor_section(x, index, 4 if s == 1 else 2 ** (7 - s))[0]
-        if s in (3, 7):
-            x = x[:, 1:]
+            x = minor_section(x, index, 4 if s == 1 else 2 ** (7 - s), keep)
     fsend[...] = fsend[...] + pack((spread_edge(x[:, 0]), spread_edge(x[:, 1])), 0)
     start_all(front_copy(k) for k in [*other, *own])
     frecv[slot // 2, slot % 2] = fsend[me]
@@ -307,18 +306,6 @@
                 delay = take_lanes(row, base + 2**j * quarter + high)
                 idx2[j - 1, low + 2 ** (CROSS - j) * high] = (lane8 - delay) & 127
 
-    def add_edge():
-        for copy in edge_copies:
-            pl.when(has_last)(copy.wait_recv)
-        x = jnp.stack([grecv[column if f == 0 else 1 - column] for f in range(2)], axis=1).reshape(32, 1, 8, 128)
-        for j in range(1, CROSS + 1):
-            x = folded_section(x, idx2[j - 1], 2 ** (CROSS - j), j == 1)
-        for k, part in enumerate([swap_halves(x[:, 0]), x[:, 1], swap_halves(x[:, 1])]):
-            extra[:, k] = part
-
-    is_late = t == NT // 2
-    pl.when(jnp.logical_not(is_late))(add_edge)
-
     for k in [*other, *own]:
         main_copy(1, k).wait_recv()
 
@@ -330,42 +317,72 @@
     x = jnp.where(jnp.broadcast_to(is_low[:, None], x.shape), 0.0, x)
     aheads = []
     for j in range(1, CROSS + 1):
-        x, ahead = major_section(x, idx2[j - 1], 2 ** (CROSS - j))
-        aheads.append(ahead)
-        if j == 3:
-            x = x[:, 1:]
+        aheads.append(x[:, -1:])
+        x = major_section(x, idx2[j - 1], 2 ** (CROSS - j), x.shape[1] - (j == 3))
     front = x
 
     high = recv[:, :, 2].reshape(32, 8, 128)
     x = jnp.stack([jnp.where(is_low, 0.0, swap_halves(high)), jnp.where(is_low, 0.0, high), *back], axis=1)
     for j in range(1, CROSS + 1):
-        x = major_section(x, idx2[j - 1], 2 ** (CROSS - j), aheads[j - 1])[0]
+        x = major_section(jnp.concatenate([aheads[j - 1], x], axis=1), idx2[j - 1], 2 ** (CROSS - j), TILES)
     norm = 16384.0 ** (-0.5)
     x = jnp.concatenate([front, x], axis=1) * norm
-    total = x[:, 1] + x[:, 2] + x[:, 3] + x[:, 4]
-    total = jnp.sum(jnp.where(is_low, 0.0, total), axis=2, keepdims=True)
-    pivot = jnp.broadcast_to(total * (1.0 / 512), (32, 8, 128))
-    pivot = pivot + swap_halves(pivot)
+    for k in range(5):
+        t2[k] = x[:, k].reshape(256, 128)
+
+    def output_rows(k, half):
+        return jnp.concatenate([t2[k, pl.ds(b * 64 + half * 4 + q, 8, stride=8), :] for q in range(4) for b in range(4)])
+
+    second = [output_rows(1 + k, 1) for k in range(TILES)]
+    pivot = jnp.sum(second[0] + second[1] + second[2] + second[3], axis=1, keepdims=True) * (1.0 / 512)
+    pivot = jnp.broadcast_to(pivot, (128, 128))
+    sums, squares = jnp.zeros((128, 128), F32), jnp.zeros((128, 128), F32)
+
+    def split(c, centred):
+        high = centred.astype(BF16)
+        low = (centred - high.astype(F32)).astype(BF16)
+        for part, value in ((hi, high), (lo, low)):
+            if c >= 0:
+                part[128 * c : 128 * c + 128, 128:256] = value
+            if c < 2 * TILES - 1:
+                part[128 * c + 128 : 128 * c + 256, 0:128] = value
+
+    for k in range(TILES):
+        ded_ref[:, 512 + 128 * k : 640 + 128 * k] = second[k]
+        centred = second[k] - pivot
+        sums, squares = sums + centred, squares + centred * centred
+        split(TILES + k, centred)
+
+    def boxcars(first, tiles):
+        at = pl.ds(128 * first, 128 * tiles)
+        both = jnp.dot(hi[at], band[...], preferred_element_type=F32)
+        both = both + jnp.dot(lo[at], band[...], preferred_element_type=F32)
+        for j in range(NBOX):
+            part = both[:, j * 128 : (j + 1) * 128].reshape(-1, 8, 128)
+            part = (part * jnp.broadcast_to(roots[1, j][None], part.shape)).reshape(tiles, 128, 128)
+            for c in range(tiles):
+                bc[first + c, j] = part[c]
 
     for k in range(NB - 1):
         front_copy(k).wait_recv()
-    y = frecv[...].reshape(32, 1, 8, 128)
+    for copy in edge_copies:
+        pl.when(has_last)(copy.wait_recv)
+    y = jnp.stack([grecv[column if f == 0 else 1 - column] for f in range(2)], axis=1).reshape(32, 8, 128)
+    y = jnp.stack([y, frecv[...].reshape(32, 8, 128)], axis=1)
     for j in range(1, CROSS + 1):
         y = folded_section(y, idx2[j - 1], 2 ** (CROSS - j), j == 1)
-    pl.when(is_late)(add_edge)
-    added = [extra[:, 0], extra[:, 1] + y[:, 0], extra[:, 2] + swap_halves(y[:, 0]), y[:, 1], swap_halves(y[:, 1])]
-    x = x + jnp.stack([jnp.where(is_low, part, 0.0) * norm for part in added], axis=1)
-    centred = x - jnp.broadcast_to(pivot[:, None], x.shape)
-    sums, squares = centred[:, 1], centred[:, 1] * centred[:, 1]
-    for k in range(2, 5):
-        sums = sums + centred[:, k]
-        squares = squares + centred[:, k] * centred[:, k]
-    sums = jnp.broadcast_to(jnp.sum(sums + swap_halves(sums), axis=2, keepdims=True), (32, 8, 128))
-    squares = jnp.broadcast_to(jnp.sum(squares + swap_halves(squares), axis=2, keepdims=True), (32, 8, 128))
+    added = [swap_halves(y[:, 0]), y[:, 1], swap_halves(y[:, 1]), y[:, 2], swap_halves(y[:, 2])]
+    for k in range(5):
+        t2[k] = (x[:, k] + jnp.where(is_low, added[k], 0.0) * norm).reshape(256, 128)
+    first = [output_rows(k, 0) for k in range(5)]
+    for k in range(1, 5):
+        centred = first[k] - pivot
+        sums, squares = sums + centred, squares + centred * centred
+    sums = jnp.broadcast_to(jnp.sum(sums, axis=1, keepdims=True), (128, 128))
+    squares = jnp.broadcast_to(jnp.sum(squares, axis=1, keepdims=True), (128, 128))
     squares = squares - sums * sums * (1.0 / 1024)
     sums = pivot + sums * (1.0 / 1024)
-    packed = jnp.where(iota((32, 8, 128), 2) == 0, sums, squares)
-    mine = jnp.transpose(packed.reshape(256, 128))[0:2]
+    mine = jnp.transpose(jnp.where(iota((128, 128), 1) == 0, sums, squares))[0:2]
     stsend[...] = mine
     stbuf[t] = mine
 
@@ -378,28 +395,11 @@
     for i in range(1, NT):
         stat_copy(i).start()
 
-    def unmix(source, first, out):
-        for k in range(TILES):
-            for s in range(8):
-                for b in range(4):
-                    rows = source[first + k, pl.ds(b * 64 + s, 8, stride=8), :]
-                    out[pl.ds(s % 4 * 32 + b * 8, 8), pl.ds(s // 4 * 512 + k * 128, 128)] = rows
-
     for k in range(5):
-        t2[k] = x[:, k].reshape(256, 128)
-        part = centred[:, k].reshape(256, 128)
-        high = part.astype(BF16)
-        hi[:, k * 128 : (k + 1) * 128] = high
-        lo[:, k * 128 : (k + 1) * 128] = (part - high.astype(F32)).astype(BF16)
-    unmix(t2, 1, ded_ref)
-    for k in range(TILES):
-        at = pl.ds(k * 128, 256)
-        both = jnp.dot(hi[:, at], band[...], preferred_element_type=F32)
-        both = both + jnp.dot(lo[:, at], band[...], preferred_element_type=F32)
-        for j in range(NBOX):
-            part = both[:, j * 128 : (j + 1) * 128].reshape(32, 8, 128)
-            bc[k, j] = (part * jnp.broadcast_to(roots[1, j][None], part.shape)).reshape(256, 128)
-
+        split(k - 1, first[k] - pivot)
+        if k:
+            ded_ref[:, 128 * k - 128 : 128 * k] = first[k]
+    boxcars(0, 2 * TILES)
     for k in range(NB - 1):
         main_copy(0, k).wait_send()
         main_copy(1, k).wait_send()
@@ -415,31 +415,26 @@
     mean = sum(means) * (1.0 / NT)
     centred = [stbuf[i][1:2] + 1024.0 * ((m - mean) * (m - mean)) for i, m in enumerate(means)]
     scale = 1.0 / jnp.sqrt(sum(centred) * (1.0 / SAMPLES) + 1e-6)
-    row_mean = jnp.transpose(jnp.broadcast_to(mean, (128, 256)))
-    row_scale = jnp.transpose(jnp.broadcast_to(scale, (128, 256)))
-    off = pivot.reshape(256, 128) - row_mean
+    row_mean = jnp.transpose(jnp.broadcast_to(mean, (128, 128)))
+    row_scale = jnp.transpose(jnp.broadcast_to(scale, (128, 128)))
+    off = pivot - row_mean
     for h in range(8):
-        at = pl.ds(32 * h, 32)
-        best = [None] * TILES
+        at = pl.ds(16 * h, 16)
+        best = [None] * (2 * TILES)
         for j in range(NBOX):
-            up = jnp.broadcast_to(roots[0, j][None], (4, 8, 128)).reshape(32, 128)
-            bias = up * off[32 * h : 32 * h + 32]
-            for k in range(TILES):
-                score = bc[k, j, at] + bias
-                best[k] = score if j == 0 else jnp.maximum(best[k], score)
-        for k in range(TILES):
-            t2[k, at] = best[k] * row_scale[32 * h : 32 * h + 32]
-    unmix(t2, 0, snr_ref)
+            up = jnp.broadcast_to(roots[0, j][None], (2, 8, 128)).reshape(16, 128)
+            bias = up * off[16 * h : 16 * h + 16]
+            for c in range(2 * TILES):
+                score = bc[c, j, at] + bias
+                best[c] = score if j == 0 else jnp.maximum(best[c], score)
+        for c in range(2 * TILES):
+            snr_ref[at, 128 * c : 128 * c + 128] = best[c] * row_scale[16 * h : 16 * h + 16]
     for i in range(1, NT):
         stat_copy(i).wait_send()
 
 
 def store(a, b, a_hbm, b_hbm, sem):
-    copies = []
-    for i, (source, target) in enumerate(((a, a_hbm), (b, b_hbm))):
-        for j in range(4):
-            at = pl.ds(32 * j, 32)
-            copies.append(pltpu.make_async_copy(source.at[at], target.at[at], sem.at[i, j]))
+    copies = [pltpu.make_async_copy(a, a_hbm, sem.at[0]), pltpu.make_async_copy(b, b_hbm, sem.at[1])]
     for copy in copies:
         copy.start()
     for copy in copies:
@@ -472,15 +467,14 @@
             vmem((32, 8, 128), F32),
             vmem((16, 2, 8, 128), F32),
             vmem((16, 2, 3, 8, 128), F32),
-            vmem((32, 3, 8, 128), F32),
             vmem((5, 256, 128), F32),
-            vmem((256, 640), BF16),
-            vmem((256, 640), BF16),
-            vmem((TILES, NBOX, 256, 128), F32),
+            vmem((1024, 256), BF16),
+            vmem((1024, 256), BF16),
+            vmem((2 * TILES, NBOX, 128, 128), F32),
             vmem((256, 1024), BF16),
             vmem((2, NBOX, 8, 128), F32),
-            vmem((2, 256), F32),
-            vmem((NT, 2, 256), F32),
+            vmem((2, 128), F32),
+            vmem((NT, 2, 128), F32),
             dma((4,)),
             dma((NB // 2,)),
             dma((NB // 2,)),
@@ -501,7 +495,7 @@
         out_shape=(out, out),
         in_specs=[in_vmem] * 2,
         out_specs=[whole] * 2,
-        scratch_shapes=[dma((2, 4))],
+        scratch_shapes=[dma((2,))],
         compiler_params=pltpu.CompilerParams(vmem_limit_bytes=52 * 2**20),
     )(ded, snr)
 

time: 36.3 us -> 36 us (level)
  no operation moved by 1% of the time
where the time goes in v3:
time: 36 us; the launch traced here: 35.9 us
  Pallas kernels  34.4 us (96%)
  local copies, waits for them, and re-layouts  0.85 us (2%)
  between operations  0.65 us (2%)
    pallas_call x1, Pallas kernels, body(): pl.pallas_call(kernel, out_shape=(out, out), in_specs=[whole, in_vmem], o...  33.4 us
    pallas_call x1, Pallas kernels, body(): pl.pallas_call(store, out_shape=(out, out), in_specs=[in_vmem] * 2, out_s...  0.99 us

profile of v3, /device:TPU:1, one launch (start us, length us, event | category | flops | bytes accessed | tf_op | source)
XLA Modules:
  0.0 35.9 jit_solution(17800392231194860729)
XLA Ops:
  0.6 0.0 copy-start
  0.6 0.7 %pad.4 = s32[16,128]{1,0:T(8,128)S(1)} pad(s32[12,128]{1,0:T(8,128)} %param.4, s32[]{:T(128)} %constant.0.clone.1), padding=0_4x0_0 | pad | bytes 14340 | tf_op jit(solution)/shard_map/jit(_pad)/pad | solution.py:449
  1.3 0.0 copy-done
  1.4 0.1 dynamic_update_slice.3.par
  1.5 33.4 %shard_map.50 = (f32[128,1024]{1,0:T(8,128)S(1)}, f32[128,1024]{1,0:T(8,128)S(1)}) custom-call(bf16[512,1024]{1,0:T(8,128)(2,1)} %x_hbm.1, s32[16,128]{1,0:T(8,128)S(1)} %dynamic_update_slice.3.par), custom_call_target="tpu_custom_call" | custom-call | tf_op jit(solution)/shard_map/pallas_call | solution.py:451
  34.9 1.0 %shard_map.51 = (f32[128,1024]{1,0:T(8,128)}, f32[128,1024]{1,0:T(8,128)}) custom-call(f32[128,1024]{1,0:T(8,128)S(1)} %get-tuple-element.4.a, f32[128,1024]{1,0:T(8,128)S(1)} %get-tuple-element.5.b), custom_call_target="tpu_custom_call" | custom-call | tf_op jit(solution)/shard_map/pallas_call | solution.py:493
Async XLA Ops:
  0.6 0.7 %copy-start = (s32[8]{0:T(128)S(1)}, s32[8]{0:T(128)}, u32[]{:S(2)}) copy-start(s32[8]{0:T(128)} %param.5) | copy-start | bytes 100

commit v4 on v3

--- a/solution.py
+++ b/solution.py
@@ -192,7 +192,7 @@
             device_id={"band": dest}, device_id_type=MESH,
         )
 
-    edges_first = t % 4 == 3
+    edges_first = t == NT // 2 - 1
 
     def start_all(copies):
         for copy in copies:

time: 36 us -> 35.9 us (level)
  no operation moved by 1% of the time
where the time goes in v4:
time: 35.9 us; the launch traced here: 35.8 us
  Pallas kernels  34.3 us (96%)
  local copies, waits for them, and re-layouts  0.85 us (2%)
  between operations  0.65 us (2%)
    pallas_call x1, Pallas kernels, body(): pl.pallas_call(kernel, out_shape=(out, out), in_specs=[whole, in_vmem], o...  33.3 us
    pallas_call x1, Pallas kernels, body(): pl.pallas_call(store, out_shape=(out, out), in_specs=[in_vmem] * 2, out_s...  0.99 us

profile of v4, /device:TPU:1, one launch (start us, length us, event | category | flops | bytes accessed | tf_op | source)
XLA Modules:
  0.0 35.8 jit_solution(8309777913129484682)
XLA Ops:
  0.6 0.0 copy-start
  0.6 0.7 %pad.4 = s32[16,128]{1,0:T(8,128)S(1)} pad(s32[12,128]{1,0:T(8,128)} %param.4, s32[]{:T(128)} %constant.0.clone.1), padding=0_4x0_0 | pad | bytes 14340 | tf_op jit(solution)/shard_map/jit(_pad)/pad | solution.py:449
  1.3 0.0 copy-done
  1.4 0.1 dynamic_update_slice.3.par
  1.5 33.3 %shard_map.50 = (f32[128,1024]{1,0:T(8,128)S(1)}, f32[128,1024]{1,0:T(8,128)S(1)}) custom-call(bf16[512,1024]{1,0:T(8,128)(2,1)} %x_hbm.1, s32[16,128]{1,0:T(8,128)S(1)} %dynamic_update_slice.3.par), custom_call_target="tpu_custom_call" | custom-call | tf_op jit(solution)/shard_map/pallas_call | solution.py:451
  34.8 1.0 %shard_map.51 = (f32[128,1024]{1,0:T(8,128)}, f32[128,1024]{1,0:T(8,128)}) custom-call(f32[128,1024]{1,0:T(8,128)S(1)} %get-tuple-element.4.a, f32[128,1024]{1,0:T(8,128)S(1)} %get-tuple-element.5.b), custom_call_target="tpu_custom_call" | custom-call | tf_op jit(solution)/shard_map/pallas_call | solution.py:493
Async XLA Ops:
  0.6 0.7 %copy-start = (s32[8]{0:T(128)S(1)}, s32[8]{0:T(128)}, u32[]{:S(2)}) copy-start(s32[8]{0:T(128)} %param.5) | copy-start | bytes 100

commit v5 on v4

--- a/solution.py
+++ b/solution.py
@@ -240,9 +240,10 @@
     tiles = local_sections(0)
     s7[:, 2] = pack(tiles, 1)
     fsend[...] = pack(tiles, 0)
-    pl.when(jnp.logical_not(edges_first))(lambda: start_all(main_copy(1, k) for k in other))
-    start_all(main_copy(1, k) for k in own)
-    pl.when(edges_first)(lambda: start_all(main_copy(1, k) for k in other))
+    pl.when(edges_first)(lambda: start_all(main_copy(1, k) for k in own[:6]))
+    start_all(main_copy(1, k) for k in other)
+    pl.when(jnp.logical_not(edges_first))(lambda: start_all(main_copy(1, k) for k in own[:6]))
+    start_all(main_copy(1, k) for k in own[6:])
     recv[slot // 2, slot % 2] = s7[me]
 
     offset, sample = iota((256, 128), 0) - 128, iota((256, 128), 1)
@@ -278,7 +279,8 @@
         else:
             x = minor_section(x, index, 4 if s == 1 else 2 ** (7 - s), keep)
     fsend[...] = fsend[...] + pack((spread_edge(x[:, 0]), spread_edge(x[:, 1])), 0)
-    start_all(front_copy(k) for k in [*other, *own])
+    hops = [2 * dx + min(dz, 8 - dz) for dx, dz, _ in OFFSETS]
+    start_all(front_copy(k) for k in sorted(range(NB - 1), key=lambda k: -hops[k]))
     frecv[slot // 2, slot % 2] = fsend[me]
 
     for e in range(2):

time: 35.9 us -> 35.6 us (level)
  Pallas kernels: 34.3 us -> 33.9 us
where the time goes in v5:
time: 35.6 us; the launch traced here: 35.4 us
  Pallas kernels  33.9 us (95%)
  local copies, waits for them, and re-layouts  0.85 us (2%)
  between operations  0.65 us (2%)
    pallas_call x1, Pallas kernels, body(): pl.pallas_call(kernel, out_shape=(out, out), in_specs=[whole, in_vmem], o...  33 us
    pallas_call x1, Pallas kernels, body(): pl.pallas_call(store, out_shape=(out, out), in_specs=[in_vmem] * 2, out_s...  0.99 us

profile of v5, /device:TPU:1, one launch (start us, length us, event | category | flops | bytes accessed | tf_op | source)
XLA Modules:
  0.0 35.4 jit_solution(5506617437866755201)
XLA Ops:
  0.6 0.0 copy-start
  0.6 0.7 %pad.4 = s32[16,128]{1,0:T(8,128)S(1)} pad(s32[12,128]{1,0:T(8,128)} %param.4, s32[]{:T(128)} %constant.0.clone.1), padding=0_4x0_0 | pad | bytes 14340 | tf_op jit(solution)/shard_map/jit(_pad)/pad | solution.py:451
  1.3 0.0 copy-done
  1.4 0.1 dynamic_update_slice.3.par
  1.5 33.0 %shard_map.50 = (f32[128,1024]{1,0:T(8,128)S(1)}, f32[128,1024]{1,0:T(8,128)S(1)}) custom-call(bf16[512,1024]{1,0:T(8,128)(2,1)} %x_hbm.1, s32[16,128]{1,0:T(8,128)S(1)} %dynamic_update_slice.3.par), custom_call_target="tpu_custom_call" | custom-call | tf_op jit(solution)/shard_map/pallas_call | solution.py:453
  34.5 1.0 %shard_map.51 = (f32[128,1024]{1,0:T(8,128)}, f32[128,1024]{1,0:T(8,128)}) custom-call(f32[128,1024]{1,0:T(8,128)S(1)} %get-tuple-element.4.a, f32[128,1024]{1,0:T(8,128)S(1)} %get-tuple-element.5.b), custom_call_target="tpu_custom_call" | custom-call | tf_op jit(solution)/shard_map/pallas_call | solution.py:495
Async XLA Ops:
  0.6 0.7 %copy-start = (s32[8]{0:T(128)S(1)}, s32[8]{0:T(128)}, u32[]{:S(2)}) copy-start(s32[8]{0:T(128)} %param.5) | copy-start | bytes 100

commit v6 on v4

--- a/solution.py
+++ b/solution.py
@@ -234,27 +234,17 @@
     s7[:, 1] = pack(tiles, 0)
     pl.semaphore_wait(barrier, NB + NT - 2)
     pl.when(has_next)(halo_copy.start)
-    for i in range(1, NB // 2):
-        shift_copy(i).start()
-    start_all(main_copy(0, k) for k in [*own, *other])
+    hops = [2 * dx + min(dz, 8 - dz) for dx, dz, _ in OFFSETS]
+    by_hops = sorted(range(NB - 1), key=lambda k: -hops[k])
+    pl.when(edges_first)(lambda: start_all(main_copy(0, k) for k in [*own, *other]))
+    pl.when(jnp.logical_not(edges_first))(lambda: start_all(main_copy(0, k) for k in by_hops))
+    start_all(shift_copy(i) for i in range(1, NB // 2))
     tiles = local_sections(0)
     s7[:, 2] = pack(tiles, 1)
     fsend[...] = pack(tiles, 0)
-    pl.when(jnp.logical_not(edges_first))(lambda: start_all(main_copy(1, k) for k in other))
-    start_all(main_copy(1, k) for k in own)
-    pl.when(edges_first)(lambda: start_all(main_copy(1, k) for k in other))
+    pl.when(edges_first)(lambda: start_all(main_copy(1, k) for k in [*own[:6], *other, *own[6:]]))
+    pl.when(jnp.logical_not(edges_first))(lambda: start_all(main_copy(1, k) for k in by_hops))
     recv[slot // 2, slot % 2] = s7[me]
-
-    offset, sample = iota((256, 128), 0) - 128, iota((256, 128), 1)
-    row = jnp.broadcast_to(par[12:13, :], (8, 128))
-    for j in range(NBOX):
-        width = take_lanes(row, jnp.full((8, 128), j, I32))
-        root = jnp.sqrt(width.astype(F32))
-        roots[0, j] = root
-        roots[1, j] = 1.0 / root
-        width = jnp.broadcast_to(width[None], (32, 8, 128)).reshape(256, 128)
-        inside = (offset <= sample) & (offset > sample - width)
-        band[:, j * 128 : (j + 1) * 128] = jnp.where(inside, 1.0, 0.0).astype(BF16)
 
     @pl.when(t == 0)
     def _():
@@ -278,13 +268,24 @@
         else:
             x = minor_section(x, index, 4 if s == 1 else 2 ** (7 - s), keep)
     fsend[...] = fsend[...] + pack((spread_edge(x[:, 0]), spread_edge(x[:, 1])), 0)
-    start_all(front_copy(k) for k in [*other, *own])
+    start_all(front_copy(k) for k in by_hops)
     frecv[slot // 2, slot % 2] = fsend[me]
 
     for e in range(2):
         for k in other if e else own:
             main_copy(0, k).wait_recv()
         pl.when(has_next)(edge_copies[e].start)
+
+    offset, sample = iota((256, 128), 0) - 128, iota((256, 128), 1)
+    row = jnp.broadcast_to(par[12:13, :], (8, 128))
+    for j in range(NBOX):
+        width = take_lanes(row, jnp.full((8, 128), j, I32))
+        root = jnp.sqrt(width.astype(F32))
+        roots[0, j] = root
+        roots[1, j] = 1.0 / root
+        width = jnp.broadcast_to(width[None], (32, 8, 128)).reshape(256, 128)
+        inside = (offset <= sample) & (offset > sample - width)
+        band[:, j * 128 : (j + 1) * 128] = jnp.where(inside, 1.0, 0.0).astype(BF16)
 
     for i in range(1, NB // 2):
         shift_copy(i).wait_recv()
@@ -328,7 +329,7 @@
     norm = 16384.0 ** (-0.5)
     x = jnp.concatenate([front, x], axis=1) * norm
     for k in range(5):
-        t2[k] = x[:, k].reshape(256, 128)
+        t2[k, 0:256] = x[:, k].reshape(256, 128)
 
     def output_rows(k, half):
         return jnp.concatenate([t2[k, pl.ds(b * 64 + half * 4 + q, 8, stride=8), :] for q in range(4) for b in range(4)])
@@ -373,7 +374,7 @@
         y = folded_section(y, idx2[j - 1], 2 ** (CROSS - j), j == 1)
     added = [swap_halves(y[:, 0]), y[:, 1], swap_halves(y[:, 1]), y[:, 2], swap_halves(y[:, 2])]
     for k in range(5):
-        t2[k] = (x[:, k] + jnp.where(is_low, added[k], 0.0) * norm).reshape(256, 128)
+        t2[k, 0:256] = (x[:, k] + jnp.where(is_low, added[k], 0.0) * norm).reshape(256, 128)
     first = [output_rows(k, 0) for k in range(5)]
     for k in range(1, 5):
         centred = first[k] - pivot
@@ -392,8 +393,7 @@
             device_id={"tm": lax.rem(t + i, NT)}, device_id_type=MESH,
         )
 
-    for i in range(1, NT):
-        stat_copy(i).start()
+    start_all(stat_copy(i) for i in (2, 6, 3, 5, 1, 7, 4))
 
     for k in range(5):
         split(k - 1, first[k] - pivot)
@@ -467,7 +467,7 @@
             vmem((32, 8, 128), F32),
             vmem((16, 2, 8, 128), F32),
             vmem((16, 2, 3, 8, 128), F32),
-            vmem((5, 256, 128), F32),
+            vmem((5, 264, 128), F32),
             vmem((1024, 256), BF16),
             vmem((1024, 256), BF16),
             vmem((2 * TILES, NBOX, 128, 128), F32),

time: 35.9 us -> 35.6 us (level)
  no operation moved by 1% of the time
where the time goes in v6:
time: 35.6 us; the launch traced here: 35.5 us
  Pallas kernels  34 us (96%)
  local copies, waits for them, and re-layouts  0.85 us (2%)
  between operations  0.65 us (2%)
    pallas_call x1, Pallas kernels, body(): pl.pallas_call(kernel, out_shape=(out, out), in_specs=[whole, in_vmem], o...  33 us
    pallas_call x1, Pallas kernels, body(): pl.pallas_call(store, out_shape=(out, out), in_specs=[in_vmem] * 2, out_s...  0.99 us

profile of v6, /device:TPU:1, one launch (start us, length us, event | category | flops | bytes accessed | tf_op | source)
XLA Modules:
  0.0 35.5 jit_solution(11813482963253045168)
XLA Ops:
  0.6 0.0 copy-start
  0.6 0.7 %pad.4 = s32[16,128]{1,0:T(8,128)S(1)} pad(s32[12,128]{1,0:T(8,128)} %param.4, s32[]{:T(128)} %constant.0.clone.1), padding=0_4x0_0 | pad | bytes 14340 | tf_op jit(solution)/shard_map/jit(_pad)/pad | solution.py:449
  1.3 0.0 copy-done
  1.4 0.1 dynamic_update_slice.3.par
  1.5 33.0 %shard_map.50 = (f32[128,1024]{1,0:T(8,128)S(1)}, f32[128,1024]{1,0:T(8,128)S(1)}) custom-call(bf16[512,1024]{1,0:T(8,128)(2,1)} %x_hbm.1, s32[16,128]{1,0:T(8,128)S(1)} %dynamic_update_slice.3.par), custom_call_target="tpu_custom_call" | custom-call | tf_op jit(solution)/shard_map/pallas_call | solution.py:451
  34.5 1.0 %shard_map.51 = (f32[128,1024]{1,0:T(8,128)}, f32[128,1024]{1,0:T(8,128)}) custom-call(f32[128,1024]{1,0:T(8,128)S(1)} %get-tuple-element.4.a, f32[128,1024]{1,0:T(8,128)S(1)} %get-tuple-element.5.b), custom_call_target="tpu_custom_call" | custom-call | tf_op jit(solution)/shard_map/pallas_call | solution.py:493
Async XLA Ops:
  0.6 0.7 %copy-start = (s32[8]{0:T(128)S(1)}, s32[8]{0:T(128)}, u32[]{:S(2)}) copy-start(s32[8]{0:T(128)} %param.5) | copy-start | bytes 100

commit v7 on v5

--- a/solution.py
+++ b/solution.py
@@ -330,7 +330,7 @@
     norm = 16384.0 ** (-0.5)
     x = jnp.concatenate([front, x], axis=1) * norm
     for k in range(5):
-        t2[k] = x[:, k].reshape(256, 128)
+        t2[k, 0:256] = x[:, k].reshape(256, 128)
 
     def output_rows(k, half):
         return jnp.concatenate([t2[k, pl.ds(b * 64 + half * 4 + q, 8, stride=8), :] for q in range(4) for b in range(4)])
@@ -375,7 +375,7 @@
         y = folded_section(y, idx2[j - 1], 2 ** (CROSS - j), j == 1)
     added = [swap_halves(y[:, 0]), y[:, 1], swap_halves(y[:, 1]), y[:, 2], swap_halves(y[:, 2])]
     for k in range(5):
-        t2[k] = (x[:, k] + jnp.where(is_low, added[k], 0.0) * norm).reshape(256, 128)
+        t2[k, 0:256] = (x[:, k] + jnp.where(is_low, added[k], 0.0) * norm).reshape(256, 128)
     first = [output_rows(k, 0) for k in range(5)]
     for k in range(1, 5):
         centred = first[k] - pivot
@@ -469,7 +469,7 @@
             vmem((32, 8, 128), F32),
             vmem((16, 2, 8, 128), F32),
             vmem((16, 2, 3, 8, 128), F32),
-            vmem((5, 256, 128), F32),
+            vmem((5, 264, 128), F32),
             vmem((1024, 256), BF16),
             vmem((1024, 256), BF16),
             vmem((2 * TILES, NBOX, 128, 128), F32),

time: 35.6 us -> 35.6 us (level)
  no operation moved by 1% of the time
where the time goes in v7:
time: 35.6 us; the launch traced here: 35.4 us
  Pallas kernels  33.9 us (95%)
  local copies, waits for them, and re-layouts  0.85 us (2%)
  between operations  0.65 us (2%)
    pallas_call x1, Pallas kernels, body(): pl.pallas_call(kernel, out_shape=(out, out), in_specs=[whole, in_vmem], o...  33 us
    pallas_call x1, Pallas kernels, body(): pl.pallas_call(store, out_shape=(out, out), in_specs=[in_vmem] * 2, out_s...  0.99 us

profile of v7, /device:TPU:1, one launch (start us, length us, event | category | flops | bytes accessed | tf_op | source)
XLA Modules:
  0.0 35.4 jit_solution(11945206902625831223)
XLA Ops:
  0.6 0.0 copy-start
  0.6 0.7 %pad.4 = s32[16,128]{1,0:T(8,128)S(1)} pad(s32[12,128]{1,0:T(8,128)} %param.4, s32[]{:T(128)} %constant.0.clone.1), padding=0_4x0_0 | pad | bytes 14340 | tf_op jit(solution)/shard_map/jit(_pad)/pad | solution.py:451
  1.3 0.0 copy-done
  1.4 0.1 dynamic_update_slice.3.par
  1.5 33.0 %shard_map.50 = (f32[128,1024]{1,0:T(8,128)S(1)}, f32[128,1024]{1,0:T(8,128)S(1)}) custom-call(bf16[512,1024]{1,0:T(8,128)(2,1)} %x_hbm.1, s32[16,128]{1,0:T(8,128)S(1)} %dynamic_update_slice.3.par), custom_call_target="tpu_custom_call" | custom-call | tf_op jit(solution)/shard_map/pallas_call | solution.py:453
  34.5 1.0 %shard_map.51 = (f32[128,1024]{1,0:T(8,128)}, f32[128,1024]{1,0:T(8,128)}) custom-call(f32[128,1024]{1,0:T(8,128)S(1)} %get-tuple-element.4.a, f32[128,1024]{1,0:T(8,128)S(1)} %get-tuple-element.5.b), custom_call_target="tpu_custom_call" | custom-call | tf_op jit(solution)/shard_map/pallas_call | solution.py:495
Async XLA Ops:
  0.6 0.7 %copy-start = (s32[8]{0:T(128)S(1)}, s32[8]{0:T(128)}, u32[]{:S(2)}) copy-start(s32[8]{0:T(128)} %param.5) | copy-start | bytes 100
